TPU v7x, 32 devices: a whole 2x2x4 slice. The times are simulated.
32 devices in a mesh: expert: 8 (over z, y), shard: 4 (over x, core).
Axes of the slice: x: 2, y: 2, z: 4, core: 2. Of those that a mesh axis runs over, the one named last changes fastest.
Arguments:
- layer_input: bfloat16 [8192, 768], P(('expert', 'shard')), may hold values from -6 to 6
- norm_gain: float32 [768], replicated, may hold values from 0.1 to 1.9
- query_weight: bfloat16 [768, 768], P(None, 'shard'), may hold values from -0.21875 to 0.21875
- key_weight: bfloat16 [768, 768], P(None, 'shard'), may hold values from -0.21875 to 0.21875
- value_weight: bfloat16 [768, 768], P(None, 'shard'), may hold values from -0.21875 to 0.21875
- output_weight: bfloat16 [768, 768], P('shard'), may hold values from -1.75 to 1.75
- bias_table: float32 [32, 12], P(None, 'shard'), may hold values from -3 to 3
- mixing_gain: float32 [768], replicated, may hold values from 0.1 to 1.9
- router_weight: float32 [768, 8], replicated, may hold values from -0.15625 to 0.15625
- up_weight: bfloat16 [8, 768, 3072], P('expert', None, 'shard'), may hold values from -0.21875 to 0.21875
- down_weight: bfloat16 [8, 3072, 768], P('expert', 'shard'), may hold values from -0.109375 to 0.109375
- expert_routes: int32 [8192, 2], P(('expert', 'shard')), may hold values from 0 to 7, all different within a row; in each aligned block of 256 rows (0 to 255, 256 to 511, ...) at most 128 rows name the same one
- cotangent: bfloat16 [8192, 768], P(('expert', 'shard')), may hold values from -6 to 6
Outputs:
- layer_output: bfloat16 [8192, 768], P(('expert', 'shard'))
- input_grad: bfloat16 [8192, 768], P(('expert', 'shard'))
- gain_grad: float32 [768], replicated
- query_grad: float32 [768, 768], P(None, 'shard')
- key_grad: float32 [768, 768], P(None, 'shard')
- value_grad: float32 [768, 768], P(None, 'shard')
- output_grad: float32 [768, 768], P('shard')
- table_grad: float32 [32, 12], P(None, 'shard')
- mixing_grad: float32 [768], replicated
- router_grad: float32 [768, 8], replicated
- up_grad: float32 [8, 768, 3072], P('expert', None, 'shard')
- down_grad: float32 [8, 3072, 768], P('expert', 'shard')
Inputs may be any that keep to these rules, and one draw needn't show every extreme that they name: `expert_routes`: each row names two different experts. Among the 256 rows of one device no expert is named by more than 128 rows, and in every draw some device has an expert named by exactly 128 of its rows.
All inputs are finite; a program needn't handle non-finite values.
Results may differ from a plain program's by a relative error of at most 0.015.
Values may be sent and summed in bfloat16 or wider, within the bound.
A program may use at most 192 MiB of HBM per device.

v0:
```python
import math

import jax
import jax.numpy as jnp
from jax import lax
from jax.sharding import PartitionSpec as P

HEAD_DIM = 64
BUCKETS = 32
MAX_DIST = 128


def gelu_tanh(values):
    return jax.nn.gelu(values, approximate=True)


def bucket_ids(distance):
    halfway = BUCKETS // 2
    far_bucket = jnp.full_like(distance, halfway)
    for bucket in range(halfway + 1, BUCKETS):
        threshold = int(math.ceil(halfway * (MAX_DIST / halfway) ** ((bucket - halfway) / halfway)))
        far_bucket = far_bucket + (distance >= threshold).astype(jnp.int32)
    return jnp.where(distance < halfway, distance, far_bucket)


def bias_rows(table_values, row_start, span, length):
    distance = jnp.arange(length, dtype=jnp.int32)
    onehot = (
        bucket_ids(distance)[:, None] == jnp.arange(BUCKETS, dtype=jnp.int32)[None, :]
    ).astype(jnp.float32)
    per_distance = jnp.dot(
        onehot, table_values, precision=lax.Precision.HIGHEST, preferred_element_type=jnp.float32
    ).T
    head_count = per_distance.shape[0]
    extended = jnp.concatenate(
        [jnp.zeros((head_count, length - 1), jnp.float32), per_distance], axis=1
    )
    window = lax.dynamic_slice_in_dim(extended, row_start, span + length - 1, 1)
    flipped = window[:, ::-1]
    stride = span + length
    repeated = jnp.tile(flipped, (1, span + 1))[:, : span * stride]
    return repeated.reshape(head_count, span, stride)[:, ::-1, :length]


def score_block(query_block, key_heads, table_values, row_start, span, length, scale):
    scores = (
        jnp.einsum("ahd,jhd->haj", query_block, key_heads, preferred_element_type=jnp.float32)
        * scale
    )
    scores = scores + bias_rows(table_values, row_start, span, length)
    position = row_start + jnp.arange(span, dtype=jnp.int32)
    causal = position[:, None] >= jnp.arange(length, dtype=jnp.int32)[None, :]
    return jnp.where(causal[None], scores, -1e30)


def on_device(
    layer_input,
    norm_gain,
    query_weight,
    key_weight,
    value_weight,
    output_weight,
    bias_table,
    mixing_gain,
    router_weight,
    up_weight,
    down_weight,
    expert_routes,
    cotangent,
):
    shard_count = lax.axis_size("shard")
    group_count = lax.axis_size("expert")
    row_count = layer_input.shape[0]
    width = layer_input.shape[1]
    length = row_count * shard_count
    local_width = query_weight.shape[1]
    head_local = local_width // HEAD_DIM
    span = min(512, length)
    scale = HEAD_DIM ** (-0.5)
    experts_all = router_weight.shape[1]
    experts_local = up_weight.shape[0]
    capacity = max(2, 4 * row_count // experts_all)

    def owner_layout(received):
        sectioned = received.reshape(group_count, experts_local, capacity, width)
        return jnp.swapaxes(sectioned, 1, 2).reshape(group_count * capacity, experts_local, width)

    def sender_layout(owner_rows):
        sectioned = owner_rows.reshape(group_count, capacity, experts_local, width)
        return jnp.swapaxes(sectioned, 1, 2).reshape(group_count, experts_local * capacity, width)

    input_values = layer_input.astype(jnp.float32)
    norm_scale = lax.rsqrt(jnp.mean(input_values * input_values, axis=-1, keepdims=True) + 1e-06)
    normed_local = (input_values * norm_scale * norm_gain).astype(jnp.bfloat16)
    normed_full = lax.all_gather(normed_local, "shard", axis=0, tiled=True)
    queries = jnp.dot(normed_full, query_weight, preferred_element_type=jnp.float32).astype(
        jnp.bfloat16
    )
    key_rows = jnp.dot(normed_full, key_weight, preferred_element_type=jnp.float32).astype(
        jnp.bfloat16
    )
    value_rows = jnp.dot(normed_full, value_weight, preferred_element_type=jnp.float32).astype(
        jnp.bfloat16
    )
    query_heads = queries.reshape(length, head_local, HEAD_DIM)
    key_heads = key_rows.reshape(length, head_local, HEAD_DIM)
    value_heads = value_rows.reshape(length, head_local, HEAD_DIM)
    starts = jnp.arange(length // span, dtype=jnp.int32) * span

    def attend_block(row_start):
        query_block = lax.dynamic_slice_in_dim(query_heads, row_start, span, 0)
        scores = score_block(query_block, key_heads, bias_table, row_start, span, length, scale)
        maximum = jnp.max(scores, axis=-1, keepdims=True)
        expo = jnp.exp(scores - maximum)
        totals = jnp.sum(expo, axis=-1, keepdims=True)
        weights = (expo / totals).astype(jnp.bfloat16)
        result = jnp.einsum(
            "haj,jhd->ahd", weights, value_heads, preferred_element_type=jnp.float32
        )
        return (
            result.reshape(span, local_width).astype(jnp.bfloat16),
            (maximum + jnp.log(totals))[..., 0],
        )

    block_out, block_lse = lax.map(attend_block, starts)
    attended = block_out.reshape(length, local_width)
    branch = lax.psum_scatter(
        jnp.dot(attended, output_weight, preferred_element_type=jnp.float32),
        "shard",
        scatter_dimension=0,
        tiled=True,
    )
    residual = input_values + branch
    mix_scale = lax.rsqrt(jnp.mean(residual * residual, axis=-1, keepdims=True) + 1e-06)
    mixed = residual * mix_scale * mixing_gain
    logits = jnp.dot(
        mixed, router_weight, precision=lax.Precision.HIGHEST, preferred_element_type=jnp.float32
    )
    route_match = expert_routes[:, :, None] == jnp.arange(experts_all, dtype=jnp.int32)
    route_hot = route_match.astype(jnp.float32)
    chosen = jnp.sum(logits[:, None, :] * route_hot, axis=-1)
    gate_probs = jax.nn.softmax(chosen, axis=-1)
    flat_match = route_match.reshape(2 * row_count, experts_all).astype(jnp.int32)
    slot_index = jnp.sum(jnp.cumsum(flat_match, axis=0) * flat_match, axis=-1) - 1
    position = (expert_routes.reshape(-1) * capacity + slot_index).reshape(row_count, 2)
    selector = (position[:, :, None] == jnp.arange(experts_all * capacity, dtype=jnp.int32)).astype(
        jnp.bfloat16
    )
    dispatched_rows = mixed.astype(jnp.bfloat16)
    send_rows = jnp.einsum(
        "tkp,td->pd", selector, dispatched_rows, preferred_element_type=jnp.float32
    ).astype(jnp.bfloat16)
    received = lax.all_to_all(
        send_rows.reshape(group_count, experts_local * capacity, width),
        "expert",
        split_axis=0,
        concat_axis=0,
        tiled=True,
    )
    expert_rows = owner_layout(received)
    rows_all = lax.all_gather(expert_rows, "shard", axis=0, tiled=True)
    hidden = jnp.einsum("red,edf->ref", rows_all, up_weight, preferred_element_type=jnp.float32)
    gelu_out, gelu_pull = jax.vjp(gelu_tanh, hidden)
    activated = gelu_out.astype(jnp.bfloat16)
    returned_rows = lax.psum_scatter(
        jnp.einsum("ref,efd->red", activated, down_weight, preferred_element_type=jnp.float32),
        "shard",
        scatter_dimension=0,
        tiled=True,
    ).astype(jnp.bfloat16)
    combined = lax.all_to_all(
        sender_layout(returned_rows), "expert", split_axis=0, concat_axis=0, tiled=True
    )
    combined_rows = combined.reshape(experts_all * capacity, width)
    picked = jnp.einsum("tkp,pd->tkd", selector, combined_rows, preferred_element_type=jnp.float32)
    mixture = jnp.sum(gate_probs[:, :, None] * picked, axis=1)
    layer_output = (residual + mixture).astype(jnp.bfloat16)
    upstream = cotangent.astype(jnp.float32)
    gate_delta = jnp.sum(upstream[:, None, :] * picked, axis=-1)
    chosen_delta = gate_probs * (
        gate_delta - jnp.sum(gate_probs * gate_delta, axis=-1, keepdims=True)
    )
    logit_delta = jnp.sum(chosen_delta[:, :, None] * route_hot, axis=1)
    router_part = jnp.einsum("td,te->de", mixed, logit_delta, precision=lax.Precision.HIGHEST)
    mixed_delta = jnp.einsum(
        "te,de->td", logit_delta, router_weight, precision=lax.Precision.HIGHEST
    )
    output_delta = (gate_probs[:, :, None] * upstream[:, None, :]).astype(jnp.bfloat16)
    back_rows = jnp.einsum(
        "tkp,tkd->pd", selector, output_delta, preferred_element_type=jnp.float32
    ).astype(jnp.bfloat16)
    returned_delta = owner_layout(
        lax.all_to_all(
            back_rows.reshape(group_count, experts_local * capacity, width),
            "expert",
            split_axis=0,
            concat_axis=0,
            tiled=True,
        )
    )
    delta_all = lax.all_gather(returned_delta, "shard", axis=0, tiled=True)
    down_grad = jnp.einsum("ref,red->efd", activated, delta_all, preferred_element_type=jnp.float32)
    activated_delta = jnp.einsum(
        "red,efd->ref", delta_all, down_weight, preferred_element_type=jnp.float32
    )
    hidden_delta = gelu_pull(activated_delta)[0].astype(jnp.bfloat16)
    up_grad = jnp.einsum("red,ref->edf", rows_all, hidden_delta, preferred_element_type=jnp.float32)
    row_delta = lax.psum_scatter(
        jnp.einsum("ref,edf->red", hidden_delta, up_weight, preferred_element_type=jnp.float32),
        "shard",
        scatter_dimension=0,
        tiled=True,
    ).astype(jnp.bfloat16)
    rows_back = lax.all_to_all(
        sender_layout(row_delta), "expert", split_axis=0, concat_axis=0, tiled=True
    )
    rows_back = rows_back.reshape(experts_all * capacity, width)
    mixed_delta = mixed_delta + jnp.einsum(
        "tkp,pd->td", selector, rows_back, preferred_element_type=jnp.float32
    )
    mix_scaled = mixed_delta * mixing_gain
    mixing_part = jnp.sum(mixed_delta * residual * mix_scale, axis=0)
    residual_delta = (
        upstream
        + mix_scale * mix_scaled
        - residual * mix_scale**3 * jnp.mean(mix_scaled * residual, axis=-1, keepdims=True)
    )
    branch_delta = lax.all_gather(residual_delta.astype(jnp.bfloat16), "shard", axis=0, tiled=True)
    output_part = jnp.einsum(
        "rc,rd->cd", attended, branch_delta, preferred_element_type=jnp.float32
    )
    attended_delta = jnp.einsum(
        "rd,cd->rc", branch_delta, output_weight, preferred_element_type=jnp.float32
    ).astype(jnp.bfloat16)
    delta_heads = attended_delta.reshape(length, head_local, HEAD_DIM)

    def back_block(carried, row_start):
        key_acc, value_acc, table_acc = carried
        query_block = lax.dynamic_slice_in_dim(query_heads, row_start, span, 0)
        delta_block = lax.dynamic_slice_in_dim(delta_heads, row_start, span, 0)
        scores = score_block(query_block, key_heads, bias_table, row_start, span, length, scale)
        lse_block = lax.dynamic_index_in_dim(block_lse, row_start // span, 0, keepdims=False)
        weights = jnp.exp(scores - lse_block[..., None])
        weight_delta = jnp.einsum(
            "ahd,jhd->haj", delta_block, value_heads, preferred_element_type=jnp.float32
        )
        centre = jnp.sum(weights * weight_delta, axis=-1, keepdims=True)
        score_delta = (weights * (weight_delta - centre)).astype(jnp.bfloat16)
        query_part = (
            jnp.einsum("haj,jhd->ahd", score_delta, key_heads, preferred_element_type=jnp.float32)
            * scale
        )
        key_acc = (
            key_acc
            + jnp.einsum(
                "haj,ahd->jhd", score_delta, query_block, preferred_element_type=jnp.float32
            )
            * scale
        )
        value_acc = value_acc + jnp.einsum(
            "haj,ahd->jhd",
            weights.astype(jnp.bfloat16),
            delta_block,
            preferred_element_type=jnp.float32,
        )
        unused, bias_pull = jax.vjp(
            lambda table_values: bias_rows(table_values, row_start, span, length), bias_table
        )
        table_acc = table_acc + bias_pull(score_delta.astype(jnp.float32))[0]
        return ((key_acc, value_acc, table_acc), query_part.reshape(span, local_width))

    zero_heads = jnp.zeros((length, head_local, HEAD_DIM), jnp.float32)
    carried, query_blocks = lax.scan(
        back_block, (zero_heads, zero_heads, jnp.zeros_like(bias_table)), starts
    )
    key_acc, value_acc, table_part = carried
    query_delta = query_blocks.reshape(length, local_width).astype(jnp.bfloat16)
    key_delta = key_acc.reshape(length, local_width).astype(jnp.bfloat16)
    value_delta = value_acc.reshape(length, local_width).astype(jnp.bfloat16)
    query_part_w = jnp.einsum(
        "rd,rc->dc", normed_full, query_delta, preferred_element_type=jnp.float32
    )
    key_part_w = jnp.einsum("rd,rc->dc", normed_full, key_delta, preferred_element_type=jnp.float32)
    value_part_w = jnp.einsum(
        "rd,rc->dc", normed_full, value_delta, preferred_element_type=jnp.float32
    )
    total = jnp.einsum("rc,dc->rd", query_delta, query_weight, preferred_element_type=jnp.float32)
    total = total + jnp.einsum(
        "rc,dc->rd", key_delta, key_weight, preferred_element_type=jnp.float32
    )
    normed_delta = lax.psum_scatter(
        (
            total
            + jnp.einsum("rc,dc->rd", value_delta, value_weight, preferred_element_type=jnp.float32)
        ).astype(jnp.bfloat16),
        "shard",
        scatter_dimension=0,
        tiled=True,
    ).astype(jnp.float32)
    gain_part = jnp.sum(normed_delta * input_values * norm_scale, axis=0)
    norm_scaled = normed_delta * norm_gain
    input_delta = (
        residual_delta
        + norm_scale * norm_scaled
        - input_values
        * norm_scale**3
        * jnp.mean(norm_scaled * input_values, axis=-1, keepdims=True)
    )
    dense = lax.psum((query_part_w, key_part_w, value_part_w, output_part, table_part), "expert")
    shared = lax.psum((gain_part, mixing_part, router_part), ("expert", "shard"))
    return (
        layer_output,
        input_delta.astype(jnp.bfloat16),
        shared[0],
        dense[0],
        dense[1],
        dense[2],
        dense[3],
        dense[4],
        shared[1],
        shared[2],
        up_grad,
        down_grad,
    )


def solution(mesh):
    return jax.shard_map(
        on_device,
        mesh=mesh,
        in_specs=(
            P(("expert", "shard"), None),
            P(),
            P(None, "shard"),
            P(None, "shard"),
            P(None, "shard"),
            P("shard", None),
            P(None, "shard"),
            P(),
            P(),
            P("expert", None, "shard"),
            P("expert", "shard", None),
            P(("expert", "shard"), None),
            P(("expert", "shard"), None),
        ),
        out_specs=(
            P(("expert", "shard"), None),
            P(("expert", "shard"), None),
            P(),
            P(None, "shard"),
            P(None, "shard"),
            P(None, "shard"),
            P("shard", None),
            P(None, "shard"),
            P(),
            P(),
            P("expert", None, "shard"),
            P("expert", "shard", None),
        ),
        check_vma=False,
    )
```

profile of v0, /device:TPU:0, one launch (start us, length us, event | category | flops | bytes accessed | tf_op | source)
XLA Modules:
  0.0 1376.7 jit_solution(2334374424230832683)
XLA Ops:
  12.2 21.9 %all-gather.5.cloned.1.call-done = bf16[1024,768]{1,0:T(8,128)(2,1)} async-done(((bf16[256,768]{1,0:T(8,128)(2,1)}), bf16[1024,768]{1,0:T(8,128)(2,1)}) %all-gather.5.cloned.1.call-update) | async-done | bytes 1572880 | tf_op jit(solution)/shard_map/all_gather | solution.py:95
  41.1 242.8 %while.31 = (s32[]{:T(128)}, bf16[2,512,192]{1,2,0:T(8,128)(2,1)S(1)}, f32[2,3,512]{2,1,0:T(4,128)}, s32[2]{0:T(128)}, bf16[1024,3,64]{0,2,1:T(8,128)(2,1)S(1)},...) while((s32[]{:T(128)}, ...), condition=%wide.region_4.5_spmd, body=%wide.region_1.4_spmd.sunk | while | flops 418691072 | bytes 138148320 | solution.py:125
  53.3 15.2 %reshape.517 = f32[2362365]{0:T(1024)} reshape(f32[3,513,1535]{2,1,0:T(8,128)} %tile.27) | data formatting | bytes 18898920 | tf_op jit(solution)/shard_map/while
  68.5 13.8 %tile.28 = f32[3,787455]{1,0:T(4,128)} reshape(f32[2362365]{0:T(1024)} %reshape.517) | data formatting | bytes 18898920 | tf_op jit(solution)/shard_map/while/body/eval_jaxpr/tile | solution.py:41
  82.4 11.0 slice.45
  93.4 7.6 copy.78
  104.4 48.5 %rev.37 = f32[3,512,1024]{2,1,0:T(8,128)} reverse(f32[3,512,1024]{2,1,0:T(8,128)} %slice.46), dimensions={1} | reverse | bytes 12582912 | tf_op jit(solution)/shard_map/while/body/eval_jaxpr/rev | solution.py:42
  174.6 15.2 %reshape.517 = f32[2362365]{0:T(1024)} reshape(f32[3,513,1535]{2,1,0:T(8,128)} %tile.27) | data formatting | bytes 18898920 | tf_op jit(solution)/shard_map/while
  189.8 13.8 %tile.28 = f32[3,787455]{1,0:T(4,128)} reshape(f32[2362365]{0:T(1024)} %reshape.517) | data formatting | bytes 18898920 | tf_op jit(solution)/shard_map/while/body/eval_jaxpr/tile | solution.py:41
  203.6 11.0 slice.45
  214.6 7.6 copy.78
  225.7 48.5 %rev.37 = f32[3,512,1024]{2,1,0:T(8,128)} reverse(f32[3,512,1024]{2,1,0:T(8,128)} %slice.46), dimensions={1} | reverse | bytes 12582912 | tf_op jit(solution)/shard_map/while/body/eval_jaxpr/rev | solution.py:42
  290.4 35.3 %reduce-scatter.5.cloned.1.call-done = f32[256,768]{1,0:T(8,128)} async-done(((f32[1024,768]{1,0:T(8,128)}), f32[256,768]{1,0:T(8,128)}) %reduce-scatter.5.cloned.1.call-update) | async-done | bytes 786448 | tf_op jit(solution)/shard_map/reduce_scatter | solution.py:127
  328.4 42.4 %all_to_all.20 = bf16[8,128,768]{2,1,0:T(8,128)(2,1)} all-to-all(bf16[8,128,768]{2,1,0:T(8,128)(2,1)S(1)} %bitcast.280), channel_id=1, replica_groups=mesh['expert'=8,'shard'=4] {'expert'}, dimensions={0} | all-to-all | bytes 3145728 | tf_op jit(solution)/shard_map/all_to_all | solution.py:153
  375.0 40.2 %all_to_all.21 = bf16[8,128,768]{2,1,0:T(8,128)(2,1)} all-to-all(bf16[8,128,768]{2,1,0:T(8,128)(2,1)S(1)} %bitcast.293), channel_id=1, replica_groups=mesh['expert'=8,'shard'=4] {'expert'}, dimensions={0} | all-to-all | bytes 3145728 | tf_op jit(solution)/shard_map/all_to_all | solution.py:193
  415.4 7.5 fusion.49
  428.9 10.3 convolution_bitcast_fusion.3
  439.3 24.0 %all-gather.9.cloned.1.call-done = bf16[4096,1,768]{2,0,1:T(8,128)(2,1)} async-done(((bf16[1024,1,768]{2,0,1:T(8,128)(2,1)}), bf16[4096,1,768]{2,0,1:T(8,128)(2,1)}) %all-gather.9.cloned.1.call-update) | async-done | bytes 6291472 | tf_op jit(solution)/shard_map/all_gather | solution.py:201
  463.3 15.5 %fusion.34 = bf16[4096,1,768]{2,0,1:T(8,128)(2,1)S(1)} fusion(f32[4096,768]{1,0:T(8,128)} %copy-done.46, bf16[1,768,768]{2,1,0:T(8,128)(2,1)S(1)} %copy-done, bf16[4096,1,768]{2,0,1:T(8,128)(2,1)} %all-gather.9.cloned.1.call-done), kind=kOutput, calls=%fused_computation.92 | convolution fusion | flops 4894752768 | bytes 26345472 | tf_op jit(solution)/shard_map/red,efd->ref/dot_general | solution.py:203
  482.6 9.7 convolution_bitcast_fusion.2
  492.3 72.7 %reduce-scatter.7.cloned.1.call-done = f32[1024,1,768]{2,0,1:T(8,128)} async-done(((f32[4096,1,768]{2,0,1:T(8,128)}), f32[1024,1,768]{2,0,1:T(8,128)}) %reduce-scatter.7.cloned.1.call-update) | async-done | bytes 3145744 | tf_op jit(solution)/shard_map/reduce_scatter | solution.py:165
  573.8 93.0 %reduce-scatter.9.cloned.1.call-done = f32[1024,1,768]{2,0,1:T(8,128)} async-done(((f32[4096,1,768]{2,0,1:T(8,128)}), f32[1024,1,768]{2,0,1:T(8,128)}) %reduce-scatter.9.cloned.1.call-update) | async-done | bytes 3145744 | tf_op jit(solution)/shard_map/reduce_scatter | solution.py:208
  678.7 34.0 %all-to-all-done.3 = bf16[8,128,768]{2,1,0:T(8,128)(2,1)} async-done(((bf16[8,128,768]{2,1,0:T(8,128)(2,1)}), bf16[8,128,768]{2,1,0:T(8,128)(2,1)}, u32[]{:S(2)}, u32[]{:S(2)}) %all-to-all-start.3) | async-done | bytes 1572896 | tf_op jit(solution)/shard_map/all_to_all | solution.py:214
  719.3 17.9 %all-gather.11.cloned.1.call-done = bf16[1024,768]{1,0:T(8,128)(2,1)} async-done(((bf16[256,768]{1,0:T(8,128)(2,1)}), bf16[1024,768]{1,0:T(8,128)(2,1)}) %all-gather.11.cloned.1.call-update) | async-done | bytes 1572880 | tf_op jit(solution)/shard_map/all_gather | solution.py:228
  739.3 472.3 %while.32 = (s32[]{:T(128)}, f32[1024,3,64]{0,2,1:T(8,128)}, f32[1024,3,64]{0,2,1:T(8,128)}, f32[32,3]{0,1:T(4,128)S(1)}, bf16[2,512,192]{1,2,0:T(8,128)(2,1)}, ...) while((s32[]{:T(128)}, f32[1024,3,64]{0,2,1:T(8,128)}, ...), condition=%wide.region_24.25_spmd.clone, body=%wide.region_21.24_spmd.clone.sunk | while | flops 1028895424 | bytes 316048640 | solution.py:273
  760.5 15.2 %reshape.518 = f32[2362365]{0:T(1024)} reshape(f32[3,513,1535]{2,1,0:T(8,128)} %tile.29) | data formatting | bytes 18898920 | tf_op jit(solution)/shard_map/while
  775.7 14.3 %tile.30 = f32[3,787455]{1,0:T(4,128)} reshape(f32[2362365]{0:T(1024)} %reshape.518) | data formatting | bytes 18898920 | tf_op jit(solution)/shard_map/while/body/eval_jaxpr/tile | solution.py:41
  794.6 6.4 copy.79
  801.0 6.6 slice.49
  807.6 48.7 %rev.38 = f32[3,512,1024]{2,1,0:T(8,128)} reverse(f32[3,512,1024]{2,1,0:T(8,128)} %slice.49), dimensions={1} | reverse | bytes 12582912 | tf_op jit(solution)/shard_map/while/body/eval_jaxpr/rev | solution.py:42
  873.6 31.7 %rev.39 = f32[3,512,1024]{2,1,0:T(8,128)} reverse(bf16[3,512,1024]{2,1,0:T(8,128)(2,1)S(1)} %multiply_convert_fusion.4), dimensions={1} | reverse | bytes 9437184 | tf_op jit(solution)/shard_map/while/body/eval_jaxpr/transpose(jvp())/rev | solution.py:42
  909.4 19.9 %copy.80 = f32[1,3,512,1536]{3,1,2,0:T(4,128)S(1)} copy(f32[1,3,512,1536]{3,2,1,0:T(8,128)S(1)} %pad_bitcast_fusion.2) | data formatting | bytes 18874368 | tf_op jit(solution)/shard_map/while
  934.3 14.1 %reshape.519 = f32[2362365]{0:T(1024)} reshape(f32[3,787455]{1,0:T(4,128)} %pad.23) | data formatting | bytes 18898920 | tf_op jit(solution)/shard_map/while
  948.4 16.3 %reshape.520 = f32[3,513,1535]{2,1,0:T(8,128)} reshape(f32[2362365]{0:T(1024)} %reshape.519) | data formatting | bytes 18898920 | tf_op jit(solution)/shard_map/while/body/eval_jaxpr/transpose(jvp())/reshape | solution.py:41
  992.4 15.2 %reshape.518 = f32[2362365]{0:T(1024)} reshape(f32[3,513,1535]{2,1,0:T(8,128)} %tile.29) | data formatting | bytes 18898920 | tf_op jit(solution)/shard_map/while
  1007.6 14.0 %tile.30 = f32[3,787455]{1,0:T(4,128)} reshape(f32[2362365]{0:T(1024)} %reshape.518) | data formatting | bytes 18898920 | tf_op jit(solution)/shard_map/while/body/eval_jaxpr/tile | solution.py:41
  1026.2 6.4 copy.79
  1032.6 6.6 slice.49
  1039.2 48.7 %rev.38 = f32[3,512,1024]{2,1,0:T(8,128)} reverse(f32[3,512,1024]{2,1,0:T(8,128)} %slice.49), dimensions={1} | reverse | bytes 12582912 | tf_op jit(solution)/shard_map/while/body/eval_jaxpr/rev | solution.py:42
  1106.4 31.7 %rev.39 = f32[3,512,1024]{2,1,0:T(8,128)} reverse(bf16[3,512,1024]{2,1,0:T(8,128)(2,1)S(1)} %multiply_convert_fusion.4), dimensions={1} | reverse | bytes 9437184 | tf_op jit(solution)/shard_map/while/body/eval_jaxpr/transpose(jvp())/rev | solution.py:42
  1142.1 19.9 %copy.80 = f32[1,3,512,1536]{3,1,2,0:T(4,128)S(1)} copy(f32[1,3,512,1536]{3,2,1,0:T(8,128)S(1)} %pad_bitcast_fusion.2) | data formatting | bytes 18874368 | tf_op jit(solution)/shard_map/while
  1167.0 14.1 %reshape.519 = f32[2362365]{0:T(1024)} reshape(f32[3,787455]{1,0:T(4,128)} %pad.23) | data formatting | bytes 18898920 | tf_op jit(solution)/shard_map/while
  1181.2 16.5 %reshape.520 = f32[3,513,1535]{2,1,0:T(8,128)} reshape(f32[2362365]{0:T(1024)} %reshape.519) | data formatting | bytes 18898920 | tf_op jit(solution)/shard_map/while/body/eval_jaxpr/transpose(jvp())/reshape | solution.py:41
  1225.9 11.8 fusion.54
  1237.8 10.2 fusion.59
  1248.7 22.4 %psum.61 = f32[32,3]{0,1:T(4,128)} all-reduce(f32[32,3]{0,1:T(4,128)S(1)} %get-tuple-element.213), channel_id=1, replica_groups=mesh['expert'=8,'shard'=4] {'expert'}, use_global_device_ids=true, to_apply=%region_33.34 | all-reduce | flops 96 | bytes 768 | tf_op jit(solution)/shard_map/psum | solution.py:309
  1272.4 38.1 %all-reduce.4 = (f32[768]{0:T(1024)}, f32[768]{0:T(1024)}, f32[768,8]{0,1:T(8,128)}) all-reduce(f32[768]{0:T(1024)S(1)} %get-tuple-element.257, f32[768]{0:T(1024)S(1)} %copy-done.40, f32[768,8]{0,1:T(8,128)S(1)} %fusion.85), channel_id=1, replica_groups=mesh['expert'=8,'shard'=4] {'expert','shard'}, use_global_device_ids=true, to_apply=%region_28.29 | all-reduce | flops 7680 | bytes 61440 | tf_op jit(solution)/shard_map/psum | solution.py:310
  1312.6 49.6 %all-reduce.8.cloned.1.call-done = (f32[768,192]{0,1:T(8,128)}, f32[768,192]{0,1:T(8,128)}, f32[768,192]{0,1:T(8,128)}, f32[192,768]{1,0:T(8,128)}) async-done(((f32[768,192]{0,1:T(8,128)}, f32[768,192]{0,1:T(8,128)}, f32[768,192]{0,1:T(8,128)}, f32[192,768]{1,0:T(8,128)}), (f32[768,192]{0,1:T(8,128)}, f32[768,192]{0,1:T(8,128)}, f32[768,192]{0,1:T(8,128)}, ...) | async-done | bytes 2359312 | tf_op jit(solution)/shard_map/psum | solution.py:309
  (289 shorter events, 240.7 us)
Async XLA Ops:
  7.2 421.7 %copy-start = (bf16[1,768,768]{2,1,0:T(8,128)(2,1)S(1)}, bf16[1,768,768]{2,1,0:T(8,128)(2,1)}, u32[]{:S(2)}) copy-start(bf16[1,768,768]{2,1,0:T(8,128)(2,1)} %param.27) | copy-start | bytes 3538948
  7.2 33.9 %copy-start.44 = (f32[32,3]{0,1:T(4,128)S(1)}, f32[32,3]{0,1:T(4,128)}, u32[]{:S(2)}) copy-start(f32[32,3]{0,1:T(4,128)} %param.23) | copy-start | bytes 1156
  7.2 26.9 %all-gather.5.cloned.1.call-start = ((), (), s32[]{:S(2)}) async-start(), calls=%async_computation.8 | async-start | bytes 1966080 | tf_op jit(solution)/shard_map/all_gather | solution.py:95
  11.6 314.2 %reduce-scatter.5.cloned.1.call-start = ((), (), s32[]{:S(2)}) async-start(), calls=%async_computation.9 | async-start | bytes 3932160 | tf_op jit(solution)/shard_map/reduce_scatter | solution.py:127
  284.0 6.4 copy-start.10
  284.0 41.8 %copy-start.15 = (bf16[256,768]{1,0:T(8,128)(2,1)S(1)}, bf16[256,768]{1,0:T(8,128)(2,1)}, u32[]{:S(2)}) copy-start(bf16[256,768]{1,0:T(8,128)(2,1)} %param.17) | copy-start | bytes 1179652
  284.0 43.7 %copy-start.28 = (f32[768]{0:T(1024)S(1)}, f32[768]{0:T(1024)}, u32[]{:S(2)}) copy-start(f32[768]{0:T(1024)} %param.24) | copy-start | bytes 9220
  284.1 6.4 copy-start.19
  287.7 84.2 %copy-start.30 = (f32[768,8]{0,1:T(8,128)S(1)}, f32[768,8]{0,1:T(8,128)}, u32[]{:S(2)}) copy-start(f32[768,8]{0,1:T(8,128)} %param.25) | copy-start | bytes 73732
  287.7 127.7 %all-gather.7.cloned.1.call-start = ((), (), s32[]{:S(2)}) async-start(), calls=%async_computation.10 | async-start | bytes 7864320 | tf_op jit(solution)/shard_map/all_gather | solution.py:161
  290.4 84.6 %copy-start.17 = (bf16[256,1024]{0,1:T(8,128)(2,1)}, bf16[256,1024]{0,1:T(8,128)(2,1)S(1)}, u32[]{:S(2)}) copy-start(bf16[256,1024]{0,1:T(8,128)(2,1)S(1)} %convert_reduce_fusion) | copy-start | bytes 1572868
  327.1 390.0 %copy-start.8 = (f32[256,768]{1,0:T(8,128)}, f32[256,768]{1,0:T(8,128)S(1)}, u32[]{:S(2)}) copy-start(f32[256,768]{1,0:T(8,128)S(1)} %get-tuple-element.309) | copy-start | bytes 2359300
  327.1 43.7 %copy-start.22 = (bf16[256,768]{1,0:T(8,128)(2,1)S(1)}, bf16[256,768]{1,0:T(8,128)(2,1)}, u32[]{:S(2)}) copy-start(bf16[256,768]{1,0:T(8,128)(2,1)} %param.29) | copy-start | bytes 1179652
  327.7 389.4 %copy-start.34 = (f32[256]{0:T(256)}, f32[256]{0:T(256)S(1)}, u32[]{:S(2)}) copy-start(f32[256]{0:T(256)S(1)} %get-tuple-element.318) | copy-start | bytes 3076
  370.8 92.5 %all-gather.9.cloned.1.call-start = ((), (), s32[]{:S(2)}) async-start(), calls=%async_computation.12 | async-start | bytes 7864320 | tf_op jit(solution)/shard_map/all_gather | solution.py:201
  372.7 50.2 %copy-start.41 = (f32[256]{0:T(256)}, f32[256]{0:T(256)S(1)}, u32[]{:S(2)}) copy-start(f32[256]{0:T(256)S(1)} %fusion.98) | copy-start | bytes 3076
  415.2 149.8 %reduce-scatter.7.cloned.1.call-start = ((), (), s32[]{:S(2)}) async-start(), calls=%async_computation.11 | async-start | bytes 15728640 | tf_op jit(solution)/shard_map/reduce_scatter | solution.py:165
  439.2 227.5 %reduce-scatter.9.cloned.1.call-start = ((), (), s32[]{:S(2)}) async-start(), calls=%async_computation.13 | async-start | bytes 15728640 | tf_op jit(solution)/shard_map/reduce_scatter | solution.py:208
  568.2 101.7 %all-to-all-start.1 = ((bf16[8,128,768]{2,1,0:T(8,128)(2,1)}), bf16[8,128,768]{2,1,0:T(8,128)(2,1)}, u32[]{:S(2)}, u32[]{:S(2)}) async-start(bf16[8,128,768]{2,1,0:T(8,128)(2,1)} %bitcast.279), calls=%async_computation.3 | async-start | bytes 3145728 | tf_op jit(solution)/shard_map/all_to_all | solution.py:171
  573.7 104.9 %copy-start.42 = (f32[256]{0:T(256)S(1)}, f32[256]{0:T(256)}, u32[]{:S(2)}) copy-start(f32[256]{0:T(256)} %copy-done.41) | copy-start | bytes 3076
  573.8 104.9 %copy-start.37 = (s32[256,2]{0,1:T(2,128)S(1)}, s32[256,2]{0,1:T(2,128)}, u32[]{:S(2)}) copy-start(s32[256,2]{0,1:T(2,128)} %param.28) | copy-start | bytes 6148
  573.8 139.0 %copy-start.18 = (bf16[256,1024]{0,1:T(8,128)(2,1)S(1)}, bf16[256,1024]{0,1:T(8,128)(2,1)}, u32[]{:S(2)}) copy-start(bf16[256,1024]{0,1:T(8,128)(2,1)} %copy-done.17) | copy-start | bytes 1572868
  670.0 47.1 %copy-start.23 = (bf16[256,768]{1,0:T(8,128)(2,1)S(1)}, bf16[256,768]{1,0:T(8,128)(2,1)}, u32[]{:S(2)}) copy-start(bf16[256,768]{1,0:T(8,128)(2,1)} %param.29) | copy-start | bytes 1179652
  670.0 42.8 %all-to-all-start.3 = ((bf16[8,128,768]{2,1,0:T(8,128)(2,1)}), bf16[8,128,768]{2,1,0:T(8,128)(2,1)}, u32[]{:S(2)}, u32[]{:S(2)}) async-start(bf16[8,128,768]{2,1,0:T(8,128)(2,1)} %bitcast.278), calls=%async_computation.6 | async-start | bytes 3145728 | tf_op jit(solution)/shard_map/all_to_all | solution.py:214
  675.6 61.6 %all-gather.11.cloned.1.call-start = ((), (), s32[]{:S(2)}) async-start(), calls=%async_computation.14 | async-start | bytes 1966080 | tf_op jit(solution)/shard_map/all_gather | solution.py:228
  678.6 60.7 %copy-start.11 = (bf16[1024,3,64]{0,2,1:T(8,128)(2,1)S(1)}, bf16[1024,3,64]{0,2,1:T(8,128)(2,1)}, u32[]{:S(2)}) copy-start(bf16[1024,3,64]{0,2,1:T(8,128)(2,1)} %copy-done.10) | copy-start | bytes 1179652
  678.7 60.6 %copy-start.31 = (f32[256,8]{0,1:T(8,128)}, f32[256,8]{0,1:T(8,128)S(1)}, u32[]{:S(2)}) copy-start(f32[256,8]{0,1:T(8,128)S(1)} %select_reduce_fusion) | copy-start | bytes 24580
  719.2 551.9 %reduce-scatter.11.cloned.1.call-start = ((), (), s32[]{:S(2)}) async-start(), calls=%async_computation.15 | async-start | bytes 1966080 | tf_op jit(solution)/shard_map/reduce_scatter | solution.py:291
  739.5 21.0 %copy-start.2 = (bf16[1024,3,64]{0,2,1:T(8,128)(2,1)}, bf16[1024,3,64]{0,2,1:T(8,128)(2,1)S(1)}, u32[]{:S(2)}) copy-start(bf16[1024,3,64]{0,2,1:T(8,128)(2,1)S(1)} %get-tuple-element.535) | copy-start | bytes 1179652 | tf_op jit(solution)/shard_map/while
  739.5 20.9 %copy-start.13 = (bf16[1024,3,64]{0,2,1:T(8,128)(2,1)}, bf16[1024,3,64]{0,2,1:T(8,128)(2,1)S(1)}, u32[]{:S(2)}) copy-start(bf16[1024,3,64]{0,2,1:T(8,128)(2,1)S(1)} %get-tuple-element.538) | copy-start | bytes 1179652 | tf_op jit(solution)/shard_map/while
  807.6 48.7 %copy-start.3 = (bf16[1024,3,64]{0,2,1:T(8,128)(2,1)S(1)}, bf16[1024,3,64]{0,2,1:T(8,128)(2,1)}, u32[]{:S(2)}) copy-start(bf16[1024,3,64]{0,2,1:T(8,128)(2,1)} %copy-done.2) | copy-start | bytes 1179652 | tf_op jit(solution)/shard_map/while
  807.6 48.7 %copy-start.5 = (pred[512,1024]{1,0:T(8,128)(4,1)S(1)}, pred[512,1024]{1,0:T(8,128)(4,1)}, u32[]{:S(2)}) copy-start(pred[512,1024]{1,0:T(8,128)(4,1)} %iota_compare_fusion.56) | copy-start | bytes 1572868 | tf_op jit(solution)/shard_map/while
  971.4 21.0 %copy-start.2 = (bf16[1024,3,64]{0,2,1:T(8,128)(2,1)}, bf16[1024,3,64]{0,2,1:T(8,128)(2,1)S(1)}, u32[]{:S(2)}) copy-start(bf16[1024,3,64]{0,2,1:T(8,128)(2,1)S(1)} %get-tuple-element.535) | copy-start | bytes 1179652 | tf_op jit(solution)/shard_map/while
  971.5 20.9 %copy-start.13 = (bf16[1024,3,64]{0,2,1:T(8,128)(2,1)}, bf16[1024,3,64]{0,2,1:T(8,128)(2,1)S(1)}, u32[]{:S(2)}) copy-start(bf16[1024,3,64]{0,2,1:T(8,128)(2,1)S(1)} %get-tuple-element.538) | copy-start | bytes 1179652 | tf_op jit(solution)/shard_map/while
  1039.2 48.7 %copy-start.3 = (bf16[1024,3,64]{0,2,1:T(8,128)(2,1)S(1)}, bf16[1024,3,64]{0,2,1:T(8,128)(2,1)}, u32[]{:S(2)}) copy-start(bf16[1024,3,64]{0,2,1:T(8,128)(2,1)} %copy-done.2) | copy-start | bytes 1179652 | tf_op jit(solution)/shard_map/while
  1039.2 48.7 %copy-start.5 = (pred[512,1024]{1,0:T(8,128)(4,1)S(1)}, pred[512,1024]{1,0:T(8,128)(4,1)}, u32[]{:S(2)}) copy-start(pred[512,1024]{1,0:T(8,128)(4,1)} %iota_compare_fusion.56) | copy-start | bytes 1572868 | tf_op jit(solution)/shard_map/while
  1219.3 143.0 %all-reduce.8.cloned.1.call-start = ((), (), s32[]{:S(2)}) async-start(), calls=%async_computation.16 | async-start | bytes 4718592 | tf_op jit(solution)/shard_map/psum | solution.py:309
  1237.7 10.3 copy-start.9
  1237.7 10.3 copy-start.29
  1237.7 10.3 copy-start.32
  1237.8 10.3 copy-start.35
  1237.8 33.3 %copy-start.16 = (bf16[256,768]{1,0:T(8,128)(2,1)S(1)}, bf16[256,768]{1,0:T(8,128)(2,1)}, u32[]{:S(2)}) copy-start(bf16[256,768]{1,0:T(8,128)(2,1)} %param.17) | copy-start | bytes 1179652
  1237.8 33.3 %copy-start.33 = (f32[768]{0:T(1024)S(1)}, f32[768]{0:T(1024)}, u32[]{:S(2)}) copy-start(f32[768]{0:T(1024)} %param.18) | copy-start | bytes 9220
  1237.8 33.3 %copy-start.39 = (f32[256]{0:T(256)S(1)}, f32[256]{0:T(256)}, u32[]{:S(2)}) copy-start(f32[256]{0:T(256)} %copy-done.38) | copy-start | bytes 3076
  1237.8 34.6 %copy-start.40 = (f32[768]{0:T(1024)S(1)}, f32[768]{0:T(1024)}, u32[]{:S(2)}) copy-start(f32[768]{0:T(1024)} %get-tuple-element.253) | copy-start | bytes 9220
  1237.8 72.8 %copy-start.21 = (f32[256,768]{1,0:T(8,128)S(1)}, f32[256,768]{1,0:T(8,128)}, u32[]{:S(2)}) copy-start(f32[256,768]{1,0:T(8,128)} %get-tuple-element.307) | copy-start | bytes 2359300
  1237.8 72.8 %copy-start.43 = (f32[256]{0:T(256)S(1)}, f32[256]{0:T(256)}, u32[]{:S(2)}) copy-start(f32[256]{0:T(256)} %get-tuple-element.315) | copy-start | bytes 3076
  1237.8 132.1 %copy-start.1 = (bf16[1,768,768]{2,1,0:T(8,128)(2,1)S(1)}, bf16[1,768,768]{2,1,0:T(8,128)(2,1)}, u32[]{:S(2)}) copy-start(bf16[1,768,768]{2,1,0:T(8,128)(2,1)} %param.27) | copy-start | bytes 3538948
  (22 other events, 87.0 us)
Sparse Core Ops, SparseCore 0:
  11.7 22.3 all-gather.4
  287.8 37.9 reduce-scatter.4
  370.9 44.4 all-gather.6
  416.9 46.3 all-gather.8
  465.9 99.0 reduce-scatter.6
  567.7 99.0 reduce-scatter.8
  719.4 17.7 all-gather.10
  1219.4 28.1 reduce-scatter.10
  1252.1 110.0 all-reduce.7
where the time goes:
time: 1390 us; the launch traced here: 1380 us
  local copies, waits for them, and re-layouts  630 us (45%)
  waiting for transfers between devices  349 us (25%)
  matrix products  153 us (11%)
  blocking collectives  143 us (10%)
  other arithmetic  49.7 us (4%)
  loops' own time  26 us (2%)
  between operations  14.8 us (1%)
    rev x6, local copies, waits for them, and re-layouts, bias_rows(): return repeated.reshape(head_count, span, stride)[:, ::-1, :length]  258 us
    while x66, local copies, waits for them, and re-layouts  175 us
    reduce_scatter x1, waiting for transfers between devices, on_device(): lax.psum_scatter(jnp.einsum('ref,edf->red', hidden_delta, up_weight, pref...  93 us
    another operation x8, local copies, waits for them, and re-layouts, bias_rows(): repeated = jnp.tile(flipped, (1, span + 1))[:, :span * stride]  75.6 us
    reduce_scatter x1, waiting for transfers between devices, on_device(): lax.psum_scatter(jnp.einsum('ref,efd->red', activated, down_weight, prefe...  72.7 us
    psum x1, waiting for transfers between devices, on_device(): lax.psum((query_part_w, key_part_w, value_part_w, output_part, table_part...  49.6 us
    all_to_all x1, blocking collectives, on_device(): lax.all_to_all(send_rows.reshape(group_count, experts_local * capacity, w...  42.4 us
    all_to_all x1, blocking collectives, on_device(): lax.all_to_all(back_rows.reshape(group_count, experts_local * capacity, w...  40.2 us
  transfers between devices with their start and end apart: 11, of which 9 were waited for; matrix products, arithmetic and copies ran while one was open for 7% of the time, Pallas kernels for 0%

commit v1 on v0

v1 whole, which is shorter than its diff:
```python
import math

import jax
import jax.numpy as jnp
from jax import lax
from jax.experimental import pallas as pl
from jax.experimental.pallas import tpu as pltpu
from jax.sharding import PartitionSpec as P

HEAD_DIM = 64
BUCKETS = 32
MAX_DIST = 128
TILE = 128
SPAN = 256
SCALE = HEAD_DIM ** (-0.5)
VMEM_BYTES = 56 * 1024 * 1024
F32 = jnp.float32
BF16 = jnp.bfloat16


def thresholds():
    halfway = BUCKETS // 2
    values = list(range(halfway + 1))
    for bucket in range(halfway + 1, BUCKETS):
        values.append(
            int(math.ceil(halfway * (MAX_DIST / halfway) ** ((bucket - halfway) / halfway)))
        )
    return values


STARTS = thresholds()


def nn(a, b):
    return lax.dot_general(a, b, (((1,), (0,)), ((), ())), preferred_element_type=F32)


def nt(a, b):
    return lax.dot_general(a, b, (((1,), (1,)), ((), ())), preferred_element_type=F32)


def tn(a, b):
    return lax.dot_general(a, b, (((0,), (0,)), ((), ())), preferred_element_type=F32)


def tile_distance():
    key = lax.broadcasted_iota(jnp.int32, (TILE, TILE), 0)
    query = lax.broadcasted_iota(jnp.int32, (TILE, TILE), 1)
    return query - key


def bias_tiles(table_ref, head):
    near = tile_distance()

    def chain(distance):
        value = jnp.full((TILE, TILE), table_ref[0, head], F32)
        for bucket in range(1, BUCKETS):
            value = jnp.where(distance >= STARTS[bucket], table_ref[bucket, head], value)
        return value

    diagonal = jnp.where(near >= 0, chain(near), -1e30)
    beside = chain(near + TILE)
    far = jnp.full((TILE, TILE), table_ref[BUCKETS - 1, head], F32)
    masked = jnp.full((TILE, TILE), -1e30, F32)
    return diagonal, beside, far, masked


def pick_tile(tiles, offset):
    if offset < 0:
        return tiles[3]
    return tiles[min(offset, 2)]


def bias_block(tiles, block):
    per = SPAN // TILE
    strips = []
    for key_tile in range(per * (block + 1)):
        strips.append(
            jnp.concatenate(
                [pick_tile(tiles, per * block + part - key_tile) for part in range(per)], axis=1
            )
        )
    return jnp.concatenate(strips, axis=0)


def attend_kernel(
    table_ref, x_ref, gain_ref, qkv_weight_ref, out_weight_ref,
    branch_ref, normed_ref, q_ref, k_ref, v_ref, att_ref, lse_ref,
):
    length = x_ref.shape[0]
    heads = q_ref.shape[0]
    local = heads * HEAD_DIM
    for block in range(length // SPAN):
        rows = slice(block * SPAN, (block + 1) * SPAN)
        x = x_ref[rows, :].astype(F32)
        norm_scale = lax.rsqrt(jnp.mean(x * x, axis=-1, keepdims=True) + 1e-06)
        normed = (x * norm_scale * gain_ref[...]).astype(BF16)
        normed_ref[rows, :] = normed
        qkv = nn(normed, qkv_weight_ref[...])
        for head in range(heads):
            cols = head * HEAD_DIM
            query = qkv[:, cols : cols + HEAD_DIM].astype(BF16)
            q_ref[head, rows, :] = (query.astype(F32) * SCALE).astype(BF16)
            k_ref[head, rows, :] = qkv[:, local + cols : local + cols + HEAD_DIM].astype(BF16)
            v_ref[head, rows, :] = qkv[:, 2 * local + cols : 2 * local + cols + HEAD_DIM].astype(
                BF16
            )
    lse_ref[...] = jnp.zeros_like(lse_ref)
    for head in range(heads):
        tiles = bias_tiles(table_ref, head)
        values_t = v_ref[head].astype(F32).T.astype(BF16)
        for block in range(length // SPAN):
            rows = slice(block * SPAN, (block + 1) * SPAN)
            reach = (block + 1) * SPAN
            scores = nt(k_ref[head, :reach, :], q_ref[head, rows, :]) + bias_block(tiles, block)
            maximum = jnp.max(scores, axis=0, keepdims=True)
            expo = jnp.exp(scores - maximum)
            totals = jnp.sum(expo, axis=0, keepdims=True)
            out_t = nn(values_t[:, :reach], expo.astype(BF16)) / totals
            att_ref[rows, head * HEAD_DIM : (head + 1) * HEAD_DIM] = out_t.T.astype(BF16)
            lse_ref[head : head + 1, rows] = maximum + jnp.log(totals)
    for block in range(length // SPAN):
        rows = slice(block * SPAN, (block + 1) * SPAN)
        branch_ref[rows, :] = nn(att_ref[rows, :], out_weight_ref[...]).astype(BF16)


def vmem_spec():
    return pl.BlockSpec(memory_space=pltpu.VMEM)


def attend(table, x_full, gain, qkv_weight, out_weight):
    length, width = x_full.shape
    local = out_weight.shape[0]
    heads = local // HEAD_DIM
    head_shape = jax.ShapeDtypeStruct((heads, length, HEAD_DIM), BF16)
    return pl.pallas_call(
        attend_kernel,
        out_shape=(
            jax.ShapeDtypeStruct((length, width), BF16),
            jax.ShapeDtypeStruct((length, width), BF16),
            head_shape,
            head_shape,
            head_shape,
            jax.ShapeDtypeStruct((length, local), BF16),
            jax.ShapeDtypeStruct((8, length), F32),
        ),
        in_specs=[pl.BlockSpec(memory_space=pltpu.SMEM)] + [vmem_spec()] * 4,
        out_specs=(vmem_spec(),) * 7,
        compiler_params=pltpu.CompilerParams(vmem_limit_bytes=VMEM_BYTES),
        cost_estimate=pl.CostEstimate(
            flops=12 * 10**9, bytes_accessed=8 * 10**6, transcendentals=2 * 10**6
        ),
        name="attend",
    )(table, x_full, gain.reshape(1, width), qkv_weight, out_weight)


def attend_back_kernel(
    table_ref, x_ref, qkv_weight_ref, out_weight_ref, q_ref, k_ref, v_ref, lse_ref, delta_ref,
    parts_ref, total_ref, gain_ref, table_grad_ref,
    att_delta_ref, key_ref, value_ref,
):
    length = x_ref.shape[0]
    heads = q_ref.shape[0]
    local = heads * HEAD_DIM
    blocks = length // SPAN
    per = SPAN // TILE
    near = tile_distance()
    for block in range(blocks):
        rows = slice(block * SPAN, (block + 1) * SPAN)
        att_delta = nt(delta_ref[rows, :], out_weight_ref[...])
        for head in range(heads):
            att_delta_ref[head, rows, :] = att_delta[
                :, head * HEAD_DIM : (head + 1) * HEAD_DIM
            ].astype(BF16)
    for head in range(heads):
        tiles = bias_tiles(table_ref, head)
        keys_t = k_ref[head].astype(F32).T.astype(BF16)
        sum_near = jnp.zeros((TILE, TILE), F32)
        sum_next = jnp.zeros((TILE, TILE), F32)
        sum_far = jnp.zeros((1, SPAN), F32)
        key_ref[...] = jnp.zeros_like(key_ref)
        value_ref[...] = jnp.zeros_like(value_ref)
        for block in range(blocks):
            rows = slice(block * SPAN, (block + 1) * SPAN)
            reach = (block + 1) * SPAN
            query = q_ref[head, rows, :]
            delta = att_delta_ref[head, rows, :]
            scores = nt(k_ref[head, :reach, :], query) + bias_block(tiles, block)
            weights = jnp.exp(scores - lse_ref[head : head + 1, rows])
            weight_delta = nt(v_ref[head, :reach, :], delta)
            centre = jnp.sum(weights * weight_delta, axis=0, keepdims=True)
            score_delta = (weights * (weight_delta - centre)).astype(BF16)
            value_ref[:reach, :] += nn(weights.astype(BF16), delta)
            key_ref[:reach, :] += nn(score_delta, query)
            query_t = nn(keys_t[:, :reach], score_delta) * SCALE
            parts_ref[rows, head * HEAD_DIM : (head + 1) * HEAD_DIM] = query_t.T.astype(BF16)
            rounded = score_delta.astype(F32)
            far_keys = max(0, (per * block - 1) * TILE)
            if far_keys:
                sum_far = sum_far + jnp.sum(rounded[:far_keys, :], axis=0, keepdims=True)
            for key_tile in range(far_keys // TILE, per * (block + 1)):
                for part in range(per):
                    offset = per * block + part - key_tile
                    if offset < 0:
                        continue
                    piece = rounded[
                        key_tile * TILE : (key_tile + 1) * TILE, part * TILE : (part + 1) * TILE
                    ]
                    if offset == 0:
                        sum_near = sum_near + piece
                    elif offset == 1:
                        sum_next = sum_next + piece
                    else:
                        total = jnp.sum(piece, axis=0, keepdims=True)
                        sum_far = sum_far + jnp.concatenate(
                            [total, jnp.zeros((1, SPAN - TILE), F32)], axis=1
                        )
        base = local + head * HEAD_DIM
        parts_ref[:, base : base + HEAD_DIM] = key_ref[...].astype(BF16)
        base = 2 * local + head * HEAD_DIM
        parts_ref[:, base : base + HEAD_DIM] = value_ref[...].astype(BF16)
        lines = []
        for bucket in range(BUCKETS):
            line = jnp.zeros((1, TILE), F32)
            for distance, sums in ((near, sum_near), (near + TILE, sum_next)):
                inside = distance >= STARTS[bucket]
                if bucket + 1 < BUCKETS:
                    inside = inside & (distance < STARTS[bucket + 1])
                line = line + jnp.sum(jnp.where(inside, sums, 0.0), axis=0, keepdims=True)
            if bucket == BUCKETS - 1:
                line = line + sum_far[:, :TILE] + sum_far[:, TILE:]
            lines.append(line)
        table_grad_ref[:, head : head + 1] = jnp.sum(
            jnp.concatenate(lines, axis=0), axis=1, keepdims=True
        )
    gain = jnp.zeros((1, x_ref.shape[1]), F32)
    for block in range(blocks):
        rows = slice(block * SPAN, (block + 1) * SPAN)
        total = nt(parts_ref[rows, :], qkv_weight_ref[...])
        x = x_ref[rows, :].astype(F32)
        norm_scale = lax.rsqrt(jnp.mean(x * x, axis=-1, keepdims=True) + 1e-06)
        gain = gain + jnp.sum(total * x * norm_scale, axis=0, keepdims=True)
        total_ref[rows, :] = total.astype(BF16)
    gain_ref[...] = gain


def attend_back(table, x_full, qkv_weight, out_weight, q, k, v, lse, delta):
    length, width = x_full.shape
    local = out_weight.shape[0]
    heads = local // HEAD_DIM
    return pl.pallas_call(
        attend_back_kernel,
        out_shape=(
            jax.ShapeDtypeStruct((length, 3 * local), BF16),
            jax.ShapeDtypeStruct((length, width), BF16),
            jax.ShapeDtypeStruct((1, width), F32),
            jax.ShapeDtypeStruct((BUCKETS, heads), F32),
        ),
        in_specs=[pl.BlockSpec(memory_space=pltpu.SMEM)] + [vmem_spec()] * 8,
        out_specs=(vmem_spec(),) * 4,
        scratch_shapes=[
            pltpu.VMEM((heads, length, HEAD_DIM), BF16),
            pltpu.VMEM((length, HEAD_DIM), F32),
            pltpu.VMEM((length, HEAD_DIM), F32),
        ],
        compiler_params=pltpu.CompilerParams(vmem_limit_bytes=VMEM_BYTES),
        cost_estimate=pl.CostEstimate(
            flops=24 * 10**9, bytes_accessed=12 * 10**6, transcendentals=2 * 10**6
        ),
        name="attend_back",
    )(table, x_full, qkv_weight, out_weight, q, k, v, lse, delta)


def experts_kernel(
    rows_ref, delta_ref, up_ref, down_ref,
    out_ref, row_delta_ref, up_grad_ref, down_grad_ref,
    out_acc, row_acc, act_ref, hid_ref,
):
    step = pl.program_id(0)
    count = rows_ref.shape[0]
    slope = math.sqrt(2.0 / math.pi)

    @pl.when(step == 0)
    def _():
        out_acc[...] = jnp.zeros_like(out_acc)
        row_acc[...] = jnp.zeros_like(row_acc)

    @pl.loop(0, count // SPAN)
    def _(block):
        rows = pl.ds(pl.multiple_of(block * SPAN, SPAN), SPAN)
        hidden = nn(rows_ref[rows, :], up_ref[0])
        square = hidden * hidden
        curve = jnp.tanh(slope * hidden * (1.0 + 0.044715 * square))
        half = 0.5 * (1.0 + curve)
        act = (hidden * half).astype(BF16)
        act_ref[rows, :] = act
        out_acc[rows, :] += nn(act, down_ref[0])
        act_delta = nt(delta_ref[rows, :], down_ref[0])
        grad = half + 0.5 * hidden * (1.0 - curve * curve) * (
            slope * (1.0 + (3 * 0.044715) * square)
        )
        hid = (grad * act_delta).astype(BF16)
        hid_ref[rows, :] = hid
        row_acc[rows, :] += nt(hid, up_ref[0])

    down_grad_ref[0] = tn(act_ref[...], delta_ref[...]).astype(BF16)
    up_grad_ref[0] = tn(rows_ref[...], hid_ref[...]).astype(BF16)

    @pl.when(step == pl.num_programs(0) - 1)
    def _():
        out_ref[...] = out_acc[...].astype(BF16)
        row_delta_ref[...] = row_acc[...].astype(BF16)


def experts(rows, delta, up, down):
    count, width = rows.shape
    chunks, _, hidden = up.shape
    flat = pl.BlockSpec((count, width), lambda c: (0, 0))
    up_block = pl.BlockSpec((1, width, hidden), lambda c: (c, 0, 0))
    down_block = pl.BlockSpec((1, hidden, width), lambda c: (c, 0, 0))
    return pl.pallas_call(
        experts_kernel,
        grid=(chunks,),
        out_shape=(
            jax.ShapeDtypeStruct((count, width), BF16),
            jax.ShapeDtypeStruct((count, width), BF16),
            jax.ShapeDtypeStruct(up.shape, BF16),
            jax.ShapeDtypeStruct(down.shape, BF16),
        ),
        in_specs=[flat, flat, up_block, down_block],
        out_specs=(flat, flat, up_block, down_block),
        scratch_shapes=[
            pltpu.VMEM((count, width), F32),
            pltpu.VMEM((count, width), F32),
            pltpu.VMEM((count, hidden), BF16),
            pltpu.VMEM((count, hidden), BF16),
        ],
        compiler_params=pltpu.CompilerParams(vmem_limit_bytes=VMEM_BYTES),
        cost_estimate=pl.CostEstimate(
            flops=12 * count * width * hidden * chunks,
            bytes_accessed=30 * 10**6,
            transcendentals=count * hidden * chunks,
        ),
        name="experts",
    )(rows, delta, up, down)


def on_device(
    layer_input,
    norm_gain,
    query_weight,
    key_weight,
    value_weight,
    output_weight,
    bias_table,
    mixing_gain,
    router_weight,
    up_weight,
    down_weight,
    expert_routes,
    cotangent,
):
    shard_count = lax.axis_size("shard")
    group_count = lax.axis_size("expert")
    shard = lax.axis_index("shard")
    group = lax.axis_index("expert")
    row_count, width = layer_input.shape
    experts_all = router_weight.shape[1]
    capacity = max(2, 4 * row_count // experts_all)
    local = output_weight.shape[0]

    x_full = lax.all_gather(layer_input, "shard", axis=0, tiled=True)
    qkv_weight = jnp.concatenate([query_weight, key_weight, value_weight], axis=1)
    x_full, early_cotangent, early_up, early_down, early_routes = lax.optimization_barrier(
        (x_full, cotangent, up_weight, down_weight, expert_routes)
    )
    up_all = lax.all_gather(early_up[0], "shard", axis=0, tiled=False)
    down_all = lax.all_gather(early_down[0], "shard", axis=0, tiled=False)
    upstream_all = lax.all_gather(early_cotangent, "expert", axis=0, tiled=False)
    routes_all = lax.all_gather(early_routes, "expert", axis=0, tiled=False)

    branch_part, normed_full, q, k, v, attended, lse = attend(
        bias_table, x_full, norm_gain, qkv_weight, output_weight
    )
    branch = lax.psum_scatter(branch_part, "shard", scatter_dimension=0, tiled=True)

    input_values = layer_input.astype(F32)
    residual = input_values + branch.astype(F32)
    mix_scale = lax.rsqrt(jnp.mean(residual * residual, axis=-1, keepdims=True) + 1e-06)
    mixed = residual * mix_scale * mixing_gain
    logits = jnp.dot(
        mixed, router_weight, precision=lax.Precision.HIGHEST, preferred_element_type=F32
    )
    route_match = expert_routes[:, :, None] == jnp.arange(experts_all, dtype=jnp.int32)
    route_hot = route_match.astype(F32)
    chosen = jnp.sum(logits[:, None, :] * route_hot, axis=-1)
    gate_probs = jax.nn.softmax(chosen, axis=-1)

    mixed_all = lax.all_gather(mixed.astype(BF16), "expert", axis=0, tiled=False)
    gates_all = lax.all_gather(gate_probs, "expert", axis=0, tiled=False)

    owned = routes_all == group
    gate_here = jnp.sum(jnp.where(owned, gates_all, 0.0), axis=-1)
    named = jnp.any(owned, axis=-1)
    slot = jnp.cumsum(named.astype(jnp.int32), axis=1) - 1
    slot = jnp.where(named, slot, -1)
    selector = (slot[:, :, None] == jnp.arange(capacity, dtype=jnp.int32)).astype(BF16)
    rows = jnp.einsum("gtc,gtd->gcd", selector, mixed_all, preferred_element_type=F32).astype(BF16)
    output_delta = (gate_here[:, :, None] * upstream_all.astype(F32)).astype(BF16)
    deltas = jnp.einsum(
        "gtc,gtd->gcd", selector, output_delta, preferred_element_type=F32
    ).astype(BF16)
    expert_out, row_delta, up_part, down_part = experts(
        rows.reshape(group_count * capacity, width),
        deltas.reshape(group_count * capacity, width),
        up_all,
        down_all,
    )
    expert_out = expert_out.reshape(group_count, capacity, width)
    row_delta = row_delta.reshape(group_count, capacity, width)
    rows_back = jnp.einsum(
        "gtc,gcd->gtd", selector, row_delta, preferred_element_type=F32
    ).astype(BF16)
    picked = jnp.einsum("gtc,gcd->gtd", selector, expert_out, preferred_element_type=F32)
    gate_delta_here = jnp.sum(upstream_all.astype(F32) * picked, axis=-1)
    share = (gate_here[:, :, None] * picked).astype(BF16)
    rows_sum = lax.psum_scatter(
        rows_back.reshape(group_count * row_count, width), "expert", scatter_dimension=0, tiled=True
    )
    gate_delta_all = lax.all_gather(gate_delta_here, "expert", axis=0, tiled=False)
    mixture = lax.psum_scatter(
        share.reshape(group_count * row_count, width), "expert", scatter_dimension=0, tiled=True
    )
    up_grad = lax.psum_scatter(up_part, "shard", scatter_dimension=0, tiled=True)
    down_grad = lax.psum_scatter(down_part, "shard", scatter_dimension=0, tiled=True)

    layer_output = (residual + mixture.astype(F32)).astype(BF16)
    upstream = cotangent.astype(F32)
    gate_delta_own = lax.dynamic_index_in_dim(gate_delta_all, group, 1, keepdims=False)
    gate_delta = jnp.sum(gate_delta_own.T[:, None, :] * route_hot, axis=-1)
    chosen_delta = gate_probs * (
        gate_delta - jnp.sum(gate_probs * gate_delta, axis=-1, keepdims=True)
    )
    logit_delta = jnp.sum(chosen_delta[:, :, None] * route_hot, axis=1)
    router_part = jnp.einsum("td,te->de", mixed, logit_delta, precision=lax.Precision.HIGHEST)
    mixed_delta = rows_sum.astype(F32) + jnp.einsum(
        "te,de->td", logit_delta, router_weight, precision=lax.Precision.HIGHEST
    )
    mix_scaled = mixed_delta * mixing_gain
    mixing_part = jnp.sum(mixed_delta * residual * mix_scale, axis=0)
    residual_delta = (
        upstream
        + mix_scale * mix_scaled
        - residual * mix_scale**3 * jnp.mean(mix_scaled * residual, axis=-1, keepdims=True)
    )
    branch_delta = lax.all_gather(residual_delta.astype(BF16), "shard", axis=0, tiled=True)
    parts, total, gain_part, table_part = attend_back(
        bias_table, x_full, qkv_weight, output_weight, q, k, v, lse, branch_delta
    )
    normed_delta = lax.psum_scatter(total, "shard", scatter_dimension=0, tiled=True).astype(F32)
    qkv_part = jnp.einsum("rd,rc->dc", normed_full, parts, preferred_element_type=F32)
    output_part = jnp.einsum("rc,rd->cd", attended, branch_delta, preferred_element_type=F32)

    norm_scale = lax.rsqrt(jnp.mean(input_values * input_values, axis=-1, keepdims=True) + 1e-06)
    norm_scaled = normed_delta * norm_gain
    input_delta = (
        residual_delta
        + norm_scale * norm_scaled
        - input_values
        * norm_scale**3
        * jnp.mean(norm_scaled * input_values, axis=-1, keepdims=True)
    )
    qkv_grad, output_grad = lax.psum(
        (qkv_part.astype(BF16), output_part.astype(BF16)), "expert"
    )
    table_hot = (jnp.arange(shard_count) == shard).astype(F32)
    table_spread = table_hot[:, None, None] * table_part[None]
    small = jnp.concatenate(
        [
            gain_part.reshape(-1),
            mixing_part,
            router_part.reshape(-1),
            table_spread.reshape(-1),
        ]
    )
    small = lax.psum(small, ("expert", "shard"))
    gain_grad = small[:width]
    mixing_grad = small[width : 2 * width]
    router_grad = small[2 * width : 2 * width + width * experts_all].reshape(width, experts_all)
    table_all = small[2 * width + width * experts_all :].reshape(table_spread.shape)
    table_grad = lax.dynamic_index_in_dim(table_all, shard, 0, keepdims=False)
    qkv_grad = qkv_grad.astype(F32)
    return (
        layer_output,
        input_delta.astype(BF16),
        gain_grad,
        qkv_grad[:, :local],
        qkv_grad[:, local : 2 * local],
        qkv_grad[:, 2 * local :],
        output_grad.astype(F32),
        table_grad,
        mixing_grad,
        router_grad,
        up_grad.astype(F32),
        down_grad.astype(F32),
    )


def solution(mesh):
    return jax.shard_map(
        on_device,
        mesh=mesh,
        in_specs=(
            P(("expert", "shard"), None),
            P(),
            P(None, "shard"),
            P(None, "shard"),
            P(None, "shard"),
            P("shard", None),
            P(None, "shard"),
            P(),
            P(),
            P("expert", None, "shard"),
            P("expert", "shard", None),
            P(("expert", "shard"), None),
            P(("expert", "shard"), None),
        ),
        out_specs=(
            P(("expert", "shard"), None),
            P(("expert", "shard"), None),
            P(),
            P(None, "shard"),
            P(None, "shard"),
            P(None, "shard"),
            P("shard", None),
            P(None, "shard"),
            P(),
            P(),
            P("expert", None, "shard"),
            P("expert", "shard", None),
        ),
        check_vma=False,
    )
```

time: 1390 us -> 722 us (0.52)
  local copies, waits for them, and re-layouts: 630 us -> 8.12 us
  matrix products: 153 us -> 27.6 us
  waiting for transfers between devices: 349 us -> 460 us
  Pallas kernels: 0 us -> 69 us
  other arithmetic: 49.7 us -> 17.9 us
  loops' own time: 26 us -> 0 us
  blocking collectives: 143 us -> 124 us
    rev x6 -> x0, local copies, waits for them, and re-layouts: 258 us -> none  [bias_rows(): return repeated.reshape(head_count, span, stride)[:, ::-1, :length]]
    while x66 -> x0, local copies, waits for them, and re-layouts: 175 us -> none
    dot_general x42 -> x6, matrix products: 149 us -> 23.1 us  [the longest x1 4.7 us: on_device(): jnp.einsum('gtc,gcd->gtd', selector, expert_out, preferred_element_type=F32)]
    all_gather x4 -> x6, waiting for transfers between devices: 63.9 us -> 170 us  [the longest x1 57.4 us: on_device(): lax.all_gather(mixed.astype(BF16), 'expert', axis=0, tiled=False)]
    all_gather x0 -> x3, blocking collectives: none -> 84.1 us  [the longest x1 31.3 us: on_device(): lax.all_gather(gate_delta_here, 'expert', axis=0, tiled=False)]
    all_to_all x2 -> x0, blocking collectives: 82.6 us -> none  [the longest x1 42.4 us: on_device(): lax.all_to_all(send_rows.reshape(group_count, experts_local * capacity, w...]
    another operation x11 -> x1, local copies, waits for them, and re-layouts: 75.6 us -> 0.01 us  [the longest x8 75.6 us: bias_rows(): repeated = jnp.tile(flipped, (1, span + 1))[:, :span * stride]]
    pallas_call x0 -> x3, Pallas kernels: none -> 69 us  [the longest x1 43.7 us: experts(): pl.pallas_call(experts_kernel, grid=(chunks,), out_shape=(jax.ShapeDtypeS...]
  transfers between devices with their start and end apart: 11 -> 13, of which waited for: 9 -> 12; matrix products, arithmetic and copies ran while one was open for 7% -> 6% of each run, Pallas kernels for 0% -> 2%
where the time goes in v1:
time: 722 us
  waiting for transfers between devices  460 us (64%)
  blocking collectives  124 us (17%)
  Pallas kernels  69 us (10%)
  matrix products  27.6 us (4%)
  other arithmetic  17.9 us (2%)
  between operations  14.3 us (2%)
  local copies, waits for them, and re-layouts  8.12 us (1%)
    psum x1, waiting for transfers between devices, on_device(): lax.psum((qkv_part.astype(BF16), output_part.astype(BF16)), 'expert')  82 us
    reduce_scatter x1, waiting for transfers between devices, on_device(): lax.psum_scatter(share.reshape(group_count * row_count, width), 'expert',...  77.1 us
    all_gather x1, waiting for transfers between devices, on_device(): lax.all_gather(mixed.astype(BF16), 'expert', axis=0, tiled=False)  57.4 us
    pallas_call x1, Pallas kernels, experts(): pl.pallas_call(experts_kernel, grid=(chunks,), out_shape=(jax.ShapeDtypeS...  43.7 us
    psum x1, blocking collectives, on_device(): small = lax.psum(small, ('expert', 'shard'))  39.8 us
    all_gather x1, waiting for transfers between devices, on_device(): down_all = lax.all_gather(early_down[0], 'shard', axis=0, tiled=False)  39 us
    reduce_scatter x1, waiting for transfers between devices, on_device(): lax.psum_scatter(rows_back.reshape(group_count * row_count, width), 'expe...  38.9 us
    all_gather x1, waiting for transfers between devices, on_device(): up_all = lax.all_gather(early_up[0], 'shard', axis=0, tiled=False)  33.6 us
  transfers between devices with their start and end apart: 13, of which 12 were waited for; matrix products, arithmetic and copies ran while one was open for 6% of the time, Pallas kernels for 2%

profile of v1, /device:TPU:0, one launch (start us, length us, event | category | flops | bytes accessed | tf_op | source)
XLA Modules:
  0.0 721.5 jit_solution(9003604163611258225)
XLA Ops:
  7.3 0.7 all-gather.11.cloned.1.call-update
  8.0 1.1 copy.76
  9.1 1.1 copy.77
  10.5 0.7 copy.79.table_ref
  11.7 1.3 pad_maximum_fusion.qkv_weight_ref
  13.1 19.0 %all-gather.11.cloned.1.call-done.x_ref = bf16[1024,768]{1,0:T(8,128)(2,1)} async-done(((bf16[256,768]{1,0:T(8,128)(2,1)}), bf16[1024,768]{1,0:T(8,128)(2,1)}) %all-gather.11.cloned.1.call-update) | async-done | bytes 1572880 | tf_op jit(solution)/shard_map/all_gather | solution.py:372
  32.0 10.8 %attend.1 = (bf16[1024,768]{1,0:T(8,128)(2,1)}, bf16[1024,768]{1,0:T(8,128)(2,1)}, bf16[3,1024,64]{2,1,0:T(8,128)(2,1)}, bf16[3,1024,64]{2,1,0:T(8,128)(2,1)}, b...) custom-call(f32[32,3]{1,0:T(8,128)} %copy.79.table_ref, ...), custom_call_target="tpu_custom_call" | custom-call | flops 12000000000 | bytes 8000000 | tf_op jit(solution)/shard_map/attend/pallas_call | solution.py:136
  42.9 0.7 all-gather.21.cloned.1.call-update
  43.7 27.6 %reduce-scatter.7.cloned.1.call-done = bf16[256,768]{1,0:T(8,128)(2,1)} async-done(((bf16[1024,768]{1,0:T(8,128)(2,1)}), bf16[256,768]{1,0:T(8,128)(2,1)}) %reduce-scatter.7.cloned.1.call-update) | async-done | bytes 393232 | tf_op jit(solution)/shard_map/reduce_scatter | solution.py:385
  71.2 1.2 multiply_reduce_fusion.2
  72.5 2.0 fusion.15
  75.7 26.2 %all-gather = s32[2048,2]{0,1:T(2,128)S(1)} all-gather(s32[256,2]{0,1:T(2,128)S(1)} %copy-done.9), channel_id=2, replica_groups=mesh['expert'=8,'shard'=4] {'expert'}, dimensions={0}, use_global_device_ids=true | all-gather | bytes 18432 | tf_op jit(solution)/shard_map/all_gather | solution.py:380
  102.0 0.6 reduce-window.6
  102.9 0.8 fusion.16
  103.9 26.7 %all_gather.43 = f32[8,256,2]{1,2,0:T(2,128)S(1)} all-gather(f32[1,256,2]{1,2,0:T(2,128)S(1)} %fusion.26), channel_id=1, replica_groups=mesh['expert'=8,'shard'=4] {'expert'}, dimensions={0}, use_global_device_ids=true | all-gather | bytes 18432 | tf_op jit(solution)/shard_map/all_gather | solution.py:400
  130.6 4.1 all-gather.21.cloned.1.call-done
  134.7 4.4 fusion.5
  139.1 57.4 %all-gather.19.cloned.1.call-done = bf16[2048,768]{1,0:T(8,128)(2,1)} async-done(((bf16[256,768]{1,0:T(8,128)(2,1)}), bf16[2048,768]{1,0:T(8,128)(2,1)}) %all-gather.19.cloned.1.call-update) | async-done | bytes 3145744 | tf_op jit(solution)/shard_map/all_gather | solution.py:399
  196.5 4.0 convolution_convert_fusion.1
  200.5 33.6 %all-gather.13.cloned.1.call-done.up_ref = bf16[4,768,768]{2,1,0:T(8,128)(2,1)} async-done(((bf16[1,768,768]{2,1,0:T(8,128)(2,1)}), bf16[4,768,768]{2,1,0:T(8,128)(2,1)}) %all-gather.13.cloned.1.call-update) | async-done | bytes 4718608 | tf_op jit(solution)/shard_map/all_gather | solution.py:377
  234.1 39.0 %all-gather.15.cloned.1.call-done.down_ref = bf16[4,768,768]{2,1,0:T(8,128)(2,1)} async-done(((bf16[1,768,768]{2,1,0:T(8,128)(2,1)}), bf16[4,768,768]{2,1,0:T(8,128)(2,1)}) %all-gather.15.cloned.1.call-update) | async-done | bytes 4718608 | tf_op jit(solution)/shard_map/all_gather | solution.py:378
  273.1 43.7 %experts.1 = (bf16[1024,768]{1,0:T(8,128)(2,1)}, bf16[1024,768]{1,0:T(8,128)(2,1)}, bf16[4,768,768]{2,1,0:T(8,128)(2,1)}, bf16[4,768,768]{2,1,0:T(8,128)(2,1)}) custom-call(bf16[1024,768]{1,0:T(8,128)(2,1)} %bitcast.44, bf16[1024,768]{1,0:T(8,128)(2,1)} %bitcast.43, bf16[4,768,768]{2,1,0:T(8,128)(2,1)} %all-gather.13.cloned.1.call-done.up_ref, ...), custom_call_target="tpu_custom_call" | custom-call | flops 28991029248 | bytes 30000000 | tf_op jit(solution)/shard_map/experts/pallas_call | solution.py:321
  316.8 3.9 convolution_convert_fusion
  320.7 4.7 fusion.1
  325.4 31.3 %all-gather.3 = f32[64,256]{1,0:T(8,128)S(1)} all-gather(f32[8,256]{1,0:T(8,128)S(1)} %get-tuple-element.109), channel_id=5, replica_groups=mesh['expert'=8,'shard'=4] {'expert'}, dimensions={0}, use_global_device_ids=true | all-gather | bytes 73728 | tf_op jit(solution)/shard_map/all_gather | solution.py:430
  356.8 38.9 %reduce-scatter.11.cloned.1.call-done = bf16[256,768]{1,0:T(8,128)(2,1)} async-done(((bf16[2048,768]{1,0:T(8,128)(2,1)}), bf16[256,768]{1,0:T(8,128)(2,1)}) %reduce-scatter.11.cloned.1.call-update) | async-done | bytes 393232 | tf_op jit(solution)/shard_map/reduce_scatter | solution.py:427
  395.7 2.2 multiply_reduce_fusion
  397.9 1.0 fusion.29
  399.0 0.7 reduce-scatter.15.cloned.1.call-update
  400.6 17.3 %all-gather.17.cloned.1.call-done.delta_ref = bf16[1024,768]{1,0:T(8,128)(2,1)} async-done(((bf16[256,768]{1,0:T(8,128)(2,1)}), bf16[1024,768]{1,0:T(8,128)(2,1)}) %all-gather.17.cloned.1.call-update) | async-done | bytes 1572880 | tf_op jit(solution)/shard_map/all_gather | solution.py:456
  417.9 2.6 convolution_convert_fusion.3
  420.5 14.5 %attend_back.1 = (bf16[1024,576]{1,0:T(8,128)(2,1)}, bf16[1024,768]{1,0:T(8,128)(2,1)}, f32[1,768]{1,0:T(1,128)}, f32[32,3]{1,0:T(8,128)}) custom-call(f32[32,3]{1,0:T(8,128)} %copy.79.table_ref, bf16[1024,768]{1,0:T(8,128)(2,1)} %all-gather.11.cloned.1.call-done.x_ref, bf16[768,576]{1,0:T(8,128)(2,1)} %pad_maximum_fusion.qkv_weight_ref, ...), custom_call_target="tpu_custom_call" | custom-call | flops 24000000000 | bytes 12000000 | tf_op jit(solution)/shard_map/attend_back/pallas_call | solution.py:251
  435.0 3.5 convolution_convert_fusion.2
  439.9 1.5 fusion.14
  441.9 39.8 %psum.21 = f32[8064]{0:T(1024)S(1)} all-reduce(f32[8064]{0:T(1024)S(1)} %pad_maximum_fusion.1), channel_id=1, replica_groups=mesh['expert'=8,'shard'=4] {'expert','shard'}, use_global_device_ids=true, to_apply=%region_20.21 | all-reduce | flops 8064 | bytes 64512 | tf_op jit(solution)/shard_map/psum | solution.py:486
  481.9 0.7 copy.85
  482.9 0.7 copy.84
  483.6 0.6 fusion.33
  484.2 2.8 convert_element_type.106
  487.0 32.4 %reduce-scatter.17.cloned.1.call-done = bf16[1,768,768]{2,1,0:T(8,128)(2,1)} async-done(((bf16[4,768,768]{2,1,0:T(8,128)(2,1)}), bf16[1,768,768]{2,1,0:T(8,128)(2,1)}) %reduce-scatter.17.cloned.1.call-update) | async-done | bytes 1179664 | tf_op jit(solution)/shard_map/reduce_scatter | solution.py:435
  519.4 2.8 convert_element_type.107
  522.3 82.0 %all-reduce.3.cloned.1.call-done = (bf16[768,576]{0,1:T(8,128)(2,1)}, bf16[192,768]{1,0:T(8,128)(2,1)}) async-done(((bf16[768,576]{0,1:T(8,128)(2,1)}, bf16[192,768]{1,0:T(8,128)(2,1)}), (bf16[768,576]{0,1:T(8,128)(2,1)}, bf16[192,768]{1,0:T(8,128)(2,1)})) %all-reduce.3.cloned.1.call-update) | async-done | bytes 1179664 | tf_op jit(solution)/shard_map/psum | solution.py:473
  604.3 1.9 convert_element_type.105
  606.2 1.2 fusion.32
  607.4 26.7 %reduce-scatter.13.cloned.1.call-done = bf16[256,768]{1,0:T(8,128)(2,1)} async-done(((bf16[1024,768]{1,0:T(8,128)(2,1)}), bf16[256,768]{1,0:T(8,128)(2,1)}) %reduce-scatter.13.cloned.1.call-update) | async-done | bytes 393232 | tf_op jit(solution)/shard_map/reduce_scatter | solution.py:460
  634.1 1.2 fusion.13
  635.3 77.1 %reduce-scatter.9.cloned.1.call-done = bf16[256,768]{1,0:T(8,128)(2,1)} async-done(((bf16[2048,768]{1,0:T(8,128)(2,1)}), bf16[256,768]{1,0:T(8,128)(2,1)}) %reduce-scatter.9.cloned.1.call-update) | async-done | bytes 393232 | tf_op jit(solution)/shard_map/reduce_scatter | solution.py:431
  712.5 2.5 fusion.12
  (89 shorter events, 6.0 us)
Async XLA Ops:
  7.2 95.7 %copy-start = (f32[768,8]{0,1:T(8,128)S(1)}, f32[768,8]{0,1:T(8,128)}, u32[]{:S(2)}) copy-start(f32[768,8]{0,1:T(8,128)} %param.21) | copy-start | bytes 73732
  7.2 3.1 copy-start.6
  7.2 3.3 copy-start.12
  7.2 4.0 copy-start.8
  7.2 24.8 %all-gather.11.cloned.1.call-start = ((), (), s32[]{:S(2)}) async-start(), calls=%async_computation.6 | async-start | bytes 1966080 | tf_op jit(solution)/shard_map/all_gather | solution.py:372
  8.0 63.3 %reduce-scatter.7.cloned.1.call-start = ((), (), s32[]{:S(2)}) async-start(), calls=%async_computation.7 | async-start | bytes 1966080 | tf_op jit(solution)/shard_map/reduce_scatter | solution.py:385
  42.8 28.4 %copy-start.2 = (bf16[256,768]{1,0:T(8,128)(2,1)S(1)}, bf16[256,768]{1,0:T(8,128)(2,1)}, u32[]{:S(2)}) copy-start(bf16[256,768]{1,0:T(8,128)(2,1)} %param.13) | copy-start | bytes 1179652
  42.8 29.6 %copy-start.7 = (f32[768]{0:T(1024)S(1)}, f32[768]{0:T(1024)}, u32[]{:S(2)}) copy-start(f32[768]{0:T(1024)} %param.20) | copy-start | bytes 9220
  42.9 91.8 %all-gather.21.cloned.1.call-start = ((), (), s32[]{:S(2)}) async-start(), calls=%async_computation.17 | async-start | bytes 3538944 | tf_op jit(solution)/shard_map/all_gather | solution.py:379
  43.6 152.9 %all-gather.19.cloned.1.call-start = ((), (), s32[]{:S(2)}) async-start(), calls=%async_computation.16 | async-start | bytes 3538944 | tf_op jit(solution)/shard_map/all_gather | solution.py:399
  72.4 3.3 copy-start.9
  72.5 30.5 %copy-start.3 = (bf16[256,768]{1,0:T(8,128)(2,1)S(1)}, bf16[256,768]{1,0:T(8,128)(2,1)}, u32[]{:S(2)}) copy-start(bf16[256,768]{1,0:T(8,128)(2,1)} %reduce-scatter.7.cloned.1.call-done) | copy-start | bytes 1179652
  74.5 159.6 %all-gather.13.cloned.1.call-start = ((), (), s32[]{:S(2)}) async-start(), calls=%async_computation.8 | async-start | bytes 5898240 | tf_op jit(solution)/shard_map/all_gather | solution.py:377
  75.1 198.0 %all-gather.15.cloned.1.call-start = ((), (), s32[]{:S(2)}) async-start(), calls=%async_computation.9 | async-start | bytes 5898240 | tf_op jit(solution)/shard_map/all_gather | solution.py:378
  75.7 320.1 %reduce-scatter.11.cloned.1.call-start = ((), (), s32[]{:S(2)}) async-start(), calls=%async_computation.11 | async-start | bytes 3538944 | tf_op jit(solution)/shard_map/reduce_scatter | solution.py:427
  320.7 97.2 %all-gather.17.cloned.1.call-start = ((), (), s32[]{:S(2)}) async-start(), calls=%async_computation.12 | async-start | bytes 1966080 | tf_op jit(solution)/shard_map/all_gather | solution.py:456
  325.4 72.5 %copy-start.5 = (bf16[256,768]{1,0:T(8,128)(2,1)S(1)}, bf16[256,768]{1,0:T(8,128)(2,1)}, u32[]{:S(2)}) copy-start(bf16[256,768]{1,0:T(8,128)(2,1)} %param.25) | copy-start | bytes 1179652
  399.0 85.2 %reduce-scatter.15.cloned.1.call-start = ((), (), s32[]{:S(2)}) async-start(), calls=%async_computation.14 | async-start | bytes 5898240 | tf_op jit(solution)/shard_map/reduce_scatter | solution.py:434
  399.7 119.7 %reduce-scatter.17.cloned.1.call-start = ((), (), s32[]{:S(2)}) async-start(), calls=%async_computation.15 | async-start | bytes 5898240 | tf_op jit(solution)/shard_map/reduce_scatter | solution.py:435
  399.8 18.1 %copy-start.13 = (bf16[1024,192]{1,0:T(8,128)(2,1)S(1)}, bf16[1024,192]{1,0:T(8,128)(2,1)}, u32[]{:S(2)}) copy-start(bf16[1024,192]{1,0:T(8,128)(2,1)} %get-tuple-element.49) | copy-start | bytes 1179652
  400.3 204.0 %all-reduce.3.cloned.1.call-start = ((), (), s32[]{:S(2)}) async-start(), calls=%async_computation.18 | async-start | bytes 2359296 | tf_op jit(solution)/shard_map/psum | solution.py:473
  420.5 14.5 %copy-start.14 = (bf16[1024,768]{1,0:T(8,128)(2,1)S(1)}, bf16[1024,768]{1,0:T(8,128)(2,1)}, u32[]{:S(2)}) copy-start(bf16[1024,768]{1,0:T(8,128)(2,1)} %get-tuple-element.47) | copy-start | bytes 4718596
  438.5 195.6 %reduce-scatter.13.cloned.1.call-start = ((), (), s32[]{:S(2)}) async-start(), calls=%async_computation.13 | async-start | bytes 1966080 | tf_op jit(solution)/shard_map/reduce_scatter | solution.py:460
  439.1 273.4 %reduce-scatter.9.cloned.1.call-start = ((), (), s32[]{:S(2)}) async-start(), calls=%async_computation.10 | async-start | bytes 3538944 | tf_op jit(solution)/shard_map/reduce_scatter | solution.py:431
  439.4 2.1 copy-start.10
  439.4 2.4 copy-start.11
  604.3 1.9 copy-start.4
  634.1 80.9 %copy-start.1 = (f32[768,8]{0,1:T(8,128)S(1)}, f32[768,8]{0,1:T(8,128)}, u32[]{:S(2)}) copy-start(f32[768,8]{0,1:T(8,128)} %param.21) | copy-start | bytes 73732
Sparse Core Ops, SparseCore 0:
  9.6 22.3 all-gather.10
  43.0 28.1 reduce-scatter.6
  73.6 60.9 all-gather.20
  137.5 58.9 all-gather.18
  198.0 36.0 all-gather.12
  235.6 37.4 all-gather.14
  320.8 74.8 reduce-scatter.10
  399.1 18.7 all-gather.16
  420.6 48.5 reduce-scatter.14
  471.5 47.8 reduce-scatter.16
  523.9 80.2 all-reduce.2
  606.7 27.4 reduce-scatter.12
  638.1 74.2 reduce-scatter.8

commit v2 on v1

--- a/solution.py
+++ b/solution.py
@@ -363,7 +363,6 @@
     shard_count = lax.axis_size("shard")
     group_count = lax.axis_size("expert")
     shard = lax.axis_index("shard")
-    group = lax.axis_index("expert")
     row_count, width = layer_input.shape
     experts_all = router_weight.shape[1]
     capacity = max(2, 4 * row_count // experts_all)
@@ -371,13 +370,9 @@
 
     x_full = lax.all_gather(layer_input, "shard", axis=0, tiled=True)
     qkv_weight = jnp.concatenate([query_weight, key_weight, value_weight], axis=1)
-    x_full, early_cotangent, early_up, early_down, early_routes = lax.optimization_barrier(
-        (x_full, cotangent, up_weight, down_weight, expert_routes)
-    )
+    x_full, early_up, early_down = lax.optimization_barrier((x_full, up_weight, down_weight))
     up_all = lax.all_gather(early_up[0], "shard", axis=0, tiled=False)
     down_all = lax.all_gather(early_down[0], "shard", axis=0, tiled=False)
-    upstream_all = lax.all_gather(early_cotangent, "expert", axis=0, tiled=False)
-    routes_all = lax.all_gather(early_routes, "expert", axis=0, tiled=False)
 
     branch_part, normed_full, q, k, v, attended, lse = attend(
         bias_table, x_full, norm_gain, qkv_weight, output_weight
@@ -396,54 +391,58 @@
     chosen = jnp.sum(logits[:, None, :] * route_hot, axis=-1)
     gate_probs = jax.nn.softmax(chosen, axis=-1)
 
-    mixed_all = lax.all_gather(mixed.astype(BF16), "expert", axis=0, tiled=False)
-    gates_all = lax.all_gather(gate_probs, "expert", axis=0, tiled=False)
-
-    owned = routes_all == group
-    gate_here = jnp.sum(jnp.where(owned, gates_all, 0.0), axis=-1)
-    named = jnp.any(owned, axis=-1)
-    slot = jnp.cumsum(named.astype(jnp.int32), axis=1) - 1
-    slot = jnp.where(named, slot, -1)
-    selector = (slot[:, :, None] == jnp.arange(capacity, dtype=jnp.int32)).astype(BF16)
-    rows = jnp.einsum("gtc,gtd->gcd", selector, mixed_all, preferred_element_type=F32).astype(BF16)
-    output_delta = (gate_here[:, :, None] * upstream_all.astype(F32)).astype(BF16)
-    deltas = jnp.einsum(
-        "gtc,gtd->gcd", selector, output_delta, preferred_element_type=F32
+    upstream = cotangent.astype(F32)
+    output_delta = (gate_probs[:, :, None] * upstream[:, None, :]).astype(BF16)
+    flat_match = route_match.reshape(2 * row_count, experts_all).astype(jnp.int32)
+    slot_index = jnp.sum(jnp.cumsum(flat_match, axis=0) * flat_match, axis=-1) - 1
+    position = (expert_routes.reshape(-1) * capacity + slot_index).reshape(row_count, 2)
+    selector = (position[:, :, None] == jnp.arange(experts_all * capacity, dtype=jnp.int32)).astype(
+        BF16
+    )
+
+    def exchange(values):
+        return lax.all_to_all(
+            values.reshape(group_count, -1, values.shape[-1]),
+            "expert",
+            split_axis=0,
+            concat_axis=0,
+            tiled=True,
+        ).reshape(values.shape)
+
+    send_rows = jnp.einsum(
+        "tkp,td->pd", selector, mixed.astype(BF16), preferred_element_type=F32
     ).astype(BF16)
-    expert_out, row_delta, up_part, down_part = experts(
-        rows.reshape(group_count * capacity, width),
-        deltas.reshape(group_count * capacity, width),
-        up_all,
-        down_all,
-    )
-    expert_out = expert_out.reshape(group_count, capacity, width)
-    row_delta = row_delta.reshape(group_count, capacity, width)
-    rows_back = jnp.einsum(
-        "gtc,gcd->gtd", selector, row_delta, preferred_element_type=F32
+    send_deltas = jnp.einsum(
+        "tkp,tkd->pd", selector, output_delta, preferred_element_type=F32
     ).astype(BF16)
-    picked = jnp.einsum("gtc,gcd->gtd", selector, expert_out, preferred_element_type=F32)
-    gate_delta_here = jnp.sum(upstream_all.astype(F32) * picked, axis=-1)
-    share = (gate_here[:, :, None] * picked).astype(BF16)
-    rows_sum = lax.psum_scatter(
-        rows_back.reshape(group_count * row_count, width), "expert", scatter_dimension=0, tiled=True
-    )
-    gate_delta_all = lax.all_gather(gate_delta_here, "expert", axis=0, tiled=False)
-    mixture = lax.psum_scatter(
-        share.reshape(group_count * row_count, width), "expert", scatter_dimension=0, tiled=True
+    rows = exchange(send_rows)
+    deltas = exchange(send_deltas)
+    expert_out, row_delta, up_part, down_part = experts(rows, deltas, up_all, down_all)
+    product = jnp.sum(deltas.astype(F32) * expert_out.astype(F32), axis=-1, keepdims=True)
+    coarse = product.astype(BF16)
+    fine = (product - coarse.astype(F32)).astype(BF16)
+    column = lax.broadcasted_iota(jnp.int32, (product.shape[0], TILE), 1)
+    beside = jnp.where(column == 0, coarse, jnp.where(column == 1, fine, jnp.zeros_like(fine)))
+    returned = exchange(jnp.concatenate([row_delta, beside], axis=1))
+    returned, late_out = lax.optimization_barrier((returned, expert_out))
+    combined = exchange(late_out)
+    rows_sum = jnp.einsum(
+        "tkp,pd->td", selector, returned[:, :width], preferred_element_type=F32
+    )
+    products = jnp.sum(
+        jnp.einsum("tkp,pc->tkc", selector, returned[:, width:], preferred_element_type=F32),
+        axis=-1,
     )
     up_grad = lax.psum_scatter(up_part, "shard", scatter_dimension=0, tiled=True)
     down_grad = lax.psum_scatter(down_part, "shard", scatter_dimension=0, tiled=True)
 
-    layer_output = (residual + mixture.astype(F32)).astype(BF16)
-    upstream = cotangent.astype(F32)
-    gate_delta_own = lax.dynamic_index_in_dim(gate_delta_all, group, 1, keepdims=False)
-    gate_delta = jnp.sum(gate_delta_own.T[:, None, :] * route_hot, axis=-1)
-    chosen_delta = gate_probs * (
-        gate_delta - jnp.sum(gate_probs * gate_delta, axis=-1, keepdims=True)
-    )
+    picked = jnp.einsum("tkp,pd->tkd", selector, combined, preferred_element_type=F32)
+    mixture = jnp.sum(gate_probs[:, :, None] * picked, axis=1)
+    layer_output = (residual + mixture).astype(BF16)
+    chosen_delta = products - gate_probs * jnp.sum(products, axis=-1, keepdims=True)
     logit_delta = jnp.sum(chosen_delta[:, :, None] * route_hot, axis=1)
     router_part = jnp.einsum("td,te->de", mixed, logit_delta, precision=lax.Precision.HIGHEST)
-    mixed_delta = rows_sum.astype(F32) + jnp.einsum(
+    mixed_delta = rows_sum + jnp.einsum(
         "te,de->td", logit_delta, router_weight, precision=lax.Precision.HIGHEST
     )
     mix_scaled = mixed_delta * mixing_gain
@@ -458,7 +457,7 @@
         bias_table, x_full, qkv_weight, output_weight, q, k, v, lse, branch_delta
     )
     normed_delta = lax.psum_scatter(total, "shard", scatter_dimension=0, tiled=True).astype(F32)
-    qkv_part = jnp.einsum("rd,rc->dc", normed_full, parts, preferred_element_type=F32)
+    qkv_part = jnp.einsum("rc,rd->cd", parts, normed_full, preferred_element_type=F32)
     output_part = jnp.einsum("rc,rd->cd", attended, branch_delta, preferred_element_type=F32)
 
     norm_scale = lax.rsqrt(jnp.mean(input_values * input_values, axis=-1, keepdims=True) + 1e-06)
@@ -470,9 +469,12 @@
         * norm_scale**3
         * jnp.mean(norm_scaled * input_values, axis=-1, keepdims=True)
     )
-    qkv_grad, output_grad = lax.psum(
-        (qkv_part.astype(BF16), output_part.astype(BF16)), "expert"
-    )
+    dense = jnp.concatenate([qkv_part.astype(BF16), output_part.astype(BF16)], axis=0)
+    dense = exchange(dense).reshape(group_count, dense.shape[0] // group_count, width)
+    dense = jnp.sum(dense.astype(F32), axis=0).astype(BF16)
+    dense = lax.all_gather(dense, "expert", axis=0, tiled=True)
+    qkv_grad = dense[: 3 * local].T
+    output_grad = dense[3 * local :]
     table_hot = (jnp.arange(shard_count) == shard).astype(F32)
     table_spread = table_hot[:, None, None] * table_part[None]
     small = jnp.concatenate(

time: 722 us -> 489 us (0.68); the launches traced: 722 us -> 480 us
  waiting for transfers between devices: 460 us -> 194 us
  starting transfers between devices: 0.99 us -> 15.3 us
  blocking collectives: 124 us -> 133 us
  matrix products: 27.6 us -> 19.6 us
    reduce_scatter x2 -> x0, waiting for transfers between devices: 116 us -> none  [the longest x1 77.1 us: on_device(): lax.psum_scatter(share.reshape(group_count * row_count, width), 'expert',...]
    all_gather x3 -> x0, blocking collectives: 84.1 us -> none  [the longest x1 31.3 us: on_device(): lax.all_gather(gate_delta_here, 'expert', axis=0, tiled=False)]
    psum x1 -> x0, waiting for transfers between devices: 82 us -> none  [on_device(): lax.psum((qkv_part.astype(BF16), output_part.astype(BF16)), 'expert')]
    all_to_all x0 -> x2, blocking collectives: none -> 80.8 us  [exchange(): lax.all_to_all(values.reshape(group_count, -1, values.shape[-1]), 'expert...]
    all_to_all x0 -> x3, waiting for transfers between devices: none -> 70.6 us  [exchange(): lax.all_to_all(values.reshape(group_count, -1, values.shape[-1]), 'expert...]
    all_gather x1, waiting for transfers between devices: 39 us -> 0.01 us  [on_device(): down_all = lax.all_gather(early_down[0], 'shard', axis=0, tiled=False)]
    all_gather x1, waiting for transfers between devices: 33.6 us -> 0.01 us  [on_device(): up_all = lax.all_gather(early_up[0], 'shard', axis=0, tiled=False)]
    reduce_scatter x1, waiting for transfers between devices: 26.7 us -> 0.02 us  [on_device(): lax.psum_scatter(total, 'shard', scatter_dimension=0, tiled=True)]
  transfers between devices with their start and end apart: 13 -> 12, of which waited for: 12 -> 7; matrix products, arithmetic and copies ran while one was open for 6% -> 8% of each run, Pallas kernels for 2% -> 0%
where the time goes in v2:
time: 489 us; the launch traced here: 480 us
  waiting for transfers between devices  194 us (40%)
  blocking collectives  133 us (27%)
  Pallas kernels  68.9 us (14%)
  other arithmetic  21.3 us (4%)
  matrix products  19.6 us (4%)
  starting transfers between devices  15.3 us (3%)
  between operations  14.8 us (3%)
  local copies, waits for them, and re-layouts  13.5 us (3%)
    all_to_all x2, blocking collectives, exchange(): lax.all_to_all(values.reshape(group_count, -1, values.shape[-1]), 'expert...  80.8 us
    all_to_all x3, waiting for transfers between devices, exchange(): lax.all_to_all(values.reshape(group_count, -1, values.shape[-1]), 'expert...  70.6 us
    psum x1, blocking collectives, on_device(): small = lax.psum(small, ('expert', 'shard'))  52.5 us
    pallas_call x1, Pallas kernels, experts(): pl.pallas_call(experts_kernel, grid=(chunks,), out_shape=(jax.ShapeDtypeS...  43.7 us
    all_gather x1, waiting for transfers between devices, on_device(): dense = lax.all_gather(dense, 'expert', axis=0, tiled=True)  41 us
    reduce_scatter x1, waiting for transfers between devices, on_device(): lax.psum_scatter(branch_part, 'shard', scatter_dimension=0, tiled=True)  25.2 us
    all_gather x1, waiting for transfers between devices, on_device(): x_full = lax.all_gather(layer_input, 'shard', axis=0, tiled=True)  18.9 us
    all_gather x1, waiting for transfers between devices, on_device(): lax.all_gather(residual_delta.astype(BF16), 'shard', axis=0, tiled=True)  17.7 us
  transfers between devices with their start and end apart: 12, of which 7 were waited for; matrix products, arithmetic and copies ran while one was open for 8% of the time, Pallas kernels for 0%

profile of v2, /device:TPU:0, one launch (start us, length us, event | category | flops | bytes accessed | tf_op | source)
XLA Modules:
  0.0 480.1 jit_solution(6982171313875820794)
XLA Ops:
  8.0 1.1 copy.86
  9.1 1.1 copy.87
  10.5 0.7 copy.89.table_ref
  11.7 1.4 pad_maximum_fusion.2.qkv_weight_ref
  13.1 18.9 %all-gather.6.cloned.1.call-done.x_ref = bf16[1024,768]{1,0:T(8,128)(2,1)} async-done(((bf16[256,768]{1,0:T(8,128)(2,1)}), bf16[1024,768]{1,0:T(8,128)(2,1)}) %all-gather.6.cloned.1.call-update) | async-done | bytes 1572880 | tf_op jit(solution)/shard_map/all_gather | solution.py:371
  32.0 10.8 %attend.1 = (bf16[1024,768]{1,0:T(8,128)(2,1)}, bf16[1024,768]{1,0:T(8,128)(2,1)}, bf16[3,1024,64]{2,1,0:T(8,128)(2,1)}, bf16[3,1024,64]{2,1,0:T(8,128)(2,1)}, b...) custom-call(f32[32,3]{1,0:T(8,128)} %copy.89.table_ref, ...), custom_call_target="tpu_custom_call" | custom-call | flops 12000000000 | bytes 8000000 | tf_op jit(solution)/shard_map/attend/pallas_call | solution.py:136
  44.1 1.1 reduce-window.6
  46.0 25.2 %reduce-scatter.5.cloned.1.call-done = bf16[256,768]{1,0:T(8,128)(2,1)} async-done(((bf16[1024,768]{1,0:T(8,128)(2,1)}), bf16[256,768]{1,0:T(8,128)(2,1)}) %reduce-scatter.5.cloned.1.call-update) | async-done | bytes 393232 | tf_op jit(solution)/shard_map/reduce_scatter | solution.py:380
  71.2 1.2 multiply_reduce_fusion.4
  72.5 1.9 fusion.18
  74.4 2.4 bitcast_convert_fusion
  76.8 5.8 %all-to-all-start.1 = ((bf16[8,128,768]{2,1,0:T(8,128)(2,1)}), bf16[8,128,768]{2,1,0:T(8,128)(2,1)S(1)}, u32[]{:S(2)}, u32[]{:S(2)}) async-start(bf16[8,128,768]{2,1,0:T(8,128)(2,1)} %bitcast.44), calls=%async_computation.2 | async-start | bytes 3145728 | tf_op jit(solution)/shard_map/all_to_all | solution.py:404
  82.9 0.8 copy-done.7
  83.7 1.9 convolution_convert_fusion
  85.6 34.0 %all-to-all-done.1 = bf16[8,128,768]{2,1,0:T(8,128)(2,1)S(1)} async-done(((bf16[8,128,768]{2,1,0:T(8,128)(2,1)}), bf16[8,128,768]{2,1,0:T(8,128)(2,1)S(1)}, u32[]{:S(2)}, u32[]{:S(2)}) %all-to-all-start.1) | async-done | bytes 1572896 | tf_op jit(solution)/shard_map/all_to_all | solution.py:404
  119.6 1.2 copy-done.4
  120.8 4.3 all-to-all-start
  125.1 36.6 %all-to-all-done = bf16[8,128,768]{2,1,0:T(8,128)(2,1)} async-done(((bf16[8,128,768]{2,1,0:T(8,128)(2,1)}), bf16[8,128,768]{2,1,0:T(8,128)(2,1)}, u32[]{:S(2)}, u32[]{:S(2)}) %all-to-all-start) | async-done | bytes 1572896 | tf_op jit(solution)/shard_map/all_to_all | solution.py:404
  161.7 43.7 %experts.1 = (bf16[1024,768]{1,0:T(8,128)(2,1)}, bf16[1024,768]{1,0:T(8,128)(2,1)}, bf16[4,768,768]{2,1,0:T(8,128)(2,1)}, bf16[4,768,768]{2,1,0:T(8,128)(2,1)}) custom-call(bf16[1024,768]{1,0:T(8,128)(2,1)} %bitcast.3.rows_ref, bf16[1024,768]{1,0:T(8,128)(2,1)} %bitcast.41, bf16[4,768,768]{2,1,0:T(8,128)(2,1)} %all-gather.8.cloned.1.call-done.up_ref, ...), custom_call_target="tpu_custom_call" | custom-call | flops 28991029248 | bytes 30000000 | tf_op jit(solution)/shard_map/experts/pallas_call | solution.py:321
  205.4 2.0 multiply_reduce_fusion
  208.0 46.2 %all_to_all.25 = bf16[8,128,896]{2,1,0:T(8,128)(2,1)S(1)} all-to-all(bf16[8,128,896]{2,1,0:T(8,128)(2,1)S(1)} %bitcast.39), channel_id=1, replica_groups=mesh['expert'=8,'shard'=4] {'expert'}, dimensions={0} | all-to-all | bytes 3670016 | tf_op jit(solution)/shard_map/all_to_all | solution.py:404
  254.1 2.4 copy.101
  256.5 1.6 fusion.33
  258.1 2.2 fusion.4
  260.4 1.2 multiply_reduce_fusion.2
  261.5 1.0 fusion.32
  262.9 17.7 %all-gather.12.cloned.1.call-done.delta_ref = bf16[1024,768]{1,0:T(8,128)(2,1)} async-done(((bf16[256,768]{1,0:T(8,128)(2,1)}), bf16[1024,768]{1,0:T(8,128)(2,1)}) %all-gather.12.cloned.1.call-update) | async-done | bytes 1572880 | tf_op jit(solution)/shard_map/all_gather | solution.py:455
  280.6 14.4 %attend_back.1 = (bf16[1024,576]{1,0:T(8,128)(2,1)}, bf16[1024,768]{1,0:T(8,128)(2,1)}, f32[1,768]{1,0:T(1,128)}, f32[32,3]{1,0:T(8,128)}) custom-call(f32[32,3]{1,0:T(8,128)} %copy.89.table_ref, bf16[1024,768]{1,0:T(8,128)(2,1)} %all-gather.6.cloned.1.call-done.x_ref, bf16[768,576]{1,0:T(8,128)(2,1)} %pad_maximum_fusion.2.qkv_weight_ref, ...), custom_call_target="tpu_custom_call" | custom-call | flops 24000000000 | bytes 12000000 | tf_op jit(solution)/shard_map/attend_back/pallas_call | solution.py:251
  295.0 0.7 reduce-scatter.9.cloned.1.call-update
  295.7 0.7 reduce-scatter.11.cloned.1.call-update
  296.8 2.0 convolution_convert_fusion.2
  298.8 2.5 convolution_convert_fusion.1
  301.4 34.6 %all_to_all.26 = bf16[8,96,768]{2,1,0:T(8,128)(2,1)S(1)} all-to-all(bf16[8,96,768]{2,1,0:T(8,128)(2,1)S(1)} %bitcast.43), channel_id=1, replica_groups=mesh['expert'=8,'shard'=4] {'expert'}, dimensions={0} | all-to-all | bytes 2359296 | tf_op jit(solution)/shard_map/all_to_all | solution.py:404
  336.0 4.6 all-to-all-start.3
  340.7 0.8 reduce_sum.156
  341.5 1.5 fusion.16
  343.6 52.5 %psum.7 = f32[8064]{0:T(1024)S(1)} all-reduce(f32[8064]{0:T(1024)S(1)} %pad_maximum_fusion.3), channel_id=1, replica_groups=mesh['expert'=8,'shard'=4] {'expert','shard'}, use_global_device_ids=true, to_apply=%region_19.20 | all-reduce | flops 8064 | bytes 64512 | tf_op jit(solution)/shard_map/psum | solution.py:488
  396.4 0.7 copy.98
  398.6 2.6 multiply_reduce_fusion.1
  401.2 1.2 fusion.13
  402.4 2.4 fusion.12
  404.8 2.8 convert_element_type.134
  407.6 17.3 %reduce-scatter.11.cloned.1.call-done = bf16[1,768,768]{2,1,0:T(8,128)(2,1)} async-done(((bf16[4,768,768]{2,1,0:T(8,128)(2,1)}), bf16[1,768,768]{2,1,0:T(8,128)(2,1)}) %reduce-scatter.11.cloned.1.call-update) | async-done | bytes 1179664 | tf_op jit(solution)/shard_map/reduce_scatter | solution.py:437
  424.9 2.8 convert_element_type.135
  427.8 41.0 %all-gather.14.cloned.1.call-done = bf16[768,768]{1,0:T(8,128)(2,1)} async-done(((bf16[96,768]{1,0:T(8,128)(2,1)}), bf16[768,768]{1,0:T(8,128)(2,1)}) %all-gather.14.cloned.1.call-update) | async-done | bytes 1179664 | tf_op jit(solution)/shard_map/all_gather | solution.py:475
  468.8 1.3 convert_bitcast_fusion
  470.1 1.2 fusion.34
  471.3 1.8 slice_convert_fusion
  (99 shorter events, 7.4 us)
Async XLA Ops:
  7.2 65.3 %copy-start = (f32[768,8]{0,1:T(8,128)S(1)}, f32[768,8]{0,1:T(8,128)}, u32[]{:S(2)}) copy-start(f32[768,8]{0,1:T(8,128)} %param.21) | copy-start | bytes 73732
  7.2 3.1 copy-start.9
  7.2 3.3 copy-start.15
  7.2 4.0 copy-start.11
  7.2 24.8 %all-gather.6.cloned.1.call-start = ((), (), s32[]{:S(2)}) async-start(), calls=%async_computation.9 | async-start | bytes 1966080 | tf_op jit(solution)/shard_map/all_gather | solution.py:371
  8.0 63.3 %reduce-scatter.5.cloned.1.call-start = ((), (), s32[]{:S(2)}) async-start(), calls=%async_computation.10 | async-start | bytes 1966080 | tf_op jit(solution)/shard_map/reduce_scatter | solution.py:380
  42.8 0.8 copy-start.12
  42.8 3.0 copy-start.6
  42.9 118.9 %all-gather.10.cloned.1.call-start = ((), (), s32[]{:S(2)}) async-start(), calls=%async_computation.12 | async-start | bytes 5898240 | tf_op jit(solution)/shard_map/all_gather | solution.py:375
  43.6 27.6 %copy-start.2 = (bf16[256,768]{1,0:T(8,128)(2,1)S(1)}, bf16[256,768]{1,0:T(8,128)(2,1)}, u32[]{:S(2)}) copy-start(bf16[256,768]{1,0:T(8,128)(2,1)} %param.13) | copy-start | bytes 1179652
  43.6 118.1 %all-gather.8.cloned.1.call-start = ((), (), s32[]{:S(2)}) async-start(), calls=%async_computation.11 | async-start | bytes 5898240 | tf_op jit(solution)/shard_map/all_gather | solution.py:374
  45.9 26.6 %copy-start.10 = (f32[768]{0:T(1024)S(1)}, f32[768]{0:T(1024)}, u32[]{:S(2)}) copy-start(f32[768]{0:T(1024)} %param.20) | copy-start | bytes 9220
  76.8 6.9 %copy-start.3 = (bf16[256,768]{1,0:T(8,128)(2,1)S(1)}, bf16[256,768]{1,0:T(8,128)(2,1)}, u32[]{:S(2)}) copy-start(bf16[256,768]{1,0:T(8,128)(2,1)} %reduce-scatter.5.cloned.1.call-done) | copy-start | bytes 1179652
  76.8 42.8 %all-to-all-start.1 = ((bf16[8,128,768]{2,1,0:T(8,128)(2,1)}), bf16[8,128,768]{2,1,0:T(8,128)(2,1)S(1)}, u32[]{:S(2)}, u32[]{:S(2)}) async-start(bf16[8,128,768]{2,1,0:T(8,128)(2,1)} %bitcast.44), calls=%async_computation.2 | async-start | bytes 3145728 | tf_op jit(solution)/shard_map/all_to_all | solution.py:404
  82.9 0.8 copy-start.7
  119.6 1.2 copy-start.4
  120.8 41.0 %all-to-all-start = ((bf16[8,128,768]{2,1,0:T(8,128)(2,1)}), bf16[8,128,768]{2,1,0:T(8,128)(2,1)}, u32[]{:S(2)}, u32[]{:S(2)}) async-start(bf16[8,128,768]{2,1,0:T(8,128)(2,1)} %bitcast.42), calls=%async_computation.1 | async-start | bytes 3145728 | tf_op jit(solution)/shard_map/all_to_all | solution.py:404
  125.1 155.5 %all-gather.12.cloned.1.call-start = ((), (), s32[]{:S(2)}) async-start(), calls=%async_computation.13 | async-start | bytes 1966080 | tf_op jit(solution)/shard_map/all_gather | solution.py:455
  161.7 43.7 %copy-start.5 = (bf16[8,128,768]{2,1,0:T(8,128)(2,1)S(1)}, bf16[8,128,768]{2,1,0:T(8,128)(2,1)}, u32[]{:S(2)}) copy-start(bf16[8,128,768]{2,1,0:T(8,128)(2,1)} %copy-done.4) | copy-start | bytes 4718596
  205.4 2.4 copy-start.8
  262.6 138.6 %reduce-scatter.7.cloned.1.call-start = ((), (), s32[]{:S(2)}) async-start(), calls=%async_computation.14 | async-start | bytes 1966080 | tf_op jit(solution)/shard_map/reduce_scatter | solution.py:459
  294.9 109.9 %reduce-scatter.9.cloned.1.call-start = ((), (), s32[]{:S(2)}) async-start(), calls=%async_computation.16 | async-start | bytes 5898240 | tf_op jit(solution)/shard_map/reduce_scatter | solution.py:436
  295.7 129.3 %reduce-scatter.11.cloned.1.call-start = ((), (), s32[]{:S(2)}) async-start(), calls=%async_computation.17 | async-start | bytes 5898240 | tf_op jit(solution)/shard_map/reduce_scatter | solution.py:437
  295.7 1.0 copy-start.16
  296.4 2.4 copy-start.17
  336.0 62.6 %all-to-all-start.3 = ((bf16[8,128,768]{2,1,0:T(8,128)(2,1)}), bf16[8,128,768]{2,1,0:T(8,128)(2,1)}, u32[]{:S(2)}, u32[]{:S(2)}) async-start(bf16[8,128,768]{2,1,0:T(8,128)(2,1)} %bitcast.9), calls=%async_computation.4 | async-start | bytes 3145728 | tf_op jit(solution)/shard_map/all_to_all | solution.py:404
  340.6 2.7 copy-start.13
  340.6 128.2 %all-gather.14.cloned.1.call-start = ((), (), s32[]{:S(2)}) async-start(), calls=%async_computation.15 | async-start | bytes 1327104 | tf_op jit(solution)/shard_map/all_gather | solution.py:475
  340.7 2.9 copy-start.14
  468.8 4.4 copy-start.1
Sparse Core Ops, SparseCore 0:
  9.6 22.3 all-gather.5
  43.0 28.1 reduce-scatter.4
  72.9 37.4 all-gather.9
  111.8 37.4 all-gather.7
  262.7 17.7 all-gather.11
  295.0 28.1 reduce-scatter.6
  325.8 48.5 reduce-scatter.8
  377.1 47.7 reduce-scatter.10
  427.7 41.0 all-gather.13
